TPU v7x, 512 devices: a whole 4x8x8 slice. The times are simulated.
512 devices in a mesh: layer: 8 (over z), row: 8 (over x, core), col: 8 (over y).
Axes of the slice: x: 4, y: 8, z: 8, core: 2. Of those that a mesh axis runs over, the one named last changes fastest.
Arguments:
- c_states: float32 [8, 64, 64, 1024], P('layer', None, 'row', 'col'), may hold values from -6 to 6
- c_adjoints: float32 [8, 64, 64, 1024], P('layer', None, 'row', 'col'), may hold values from -6 to 6
- weights: bfloat16 [32, 64, 576], P('layer'), may hold values from -0.25 to 0.25
Outputs:
- new_states: float32 [8, 64, 64, 1024], P('layer', None, 'row', 'col')
- new_adjoints: float32 [8, 64, 64, 1024], P('layer', None, 'row', 'col')
- weight_grads: float32 [32, 64, 576], P('layer')
All inputs are finite; a program needn't handle non-finite values.
Results may differ from a plain program's by a relative error of at most 0.006.
Values may be sent and summed in bfloat16 or wider, within the bound.
A program may use at most 64 MiB of HBM per device.

v0:
```python
import jax
import jax.numpy as jnp
from jax import lax
from jax.sharding import PartitionSpec as P

step_size = 0.2


def with_halo(cells, sides, width):
    for axis, dim in sides:
        count = lax.axis_size(axis)
        ends = count - 1
        head = lax.slice_in_dim(cells, 0, width, axis=dim)
        tail = lax.slice_in_dim(cells, cells.shape[dim] - width, cells.shape[dim], axis=dim)
        cells = jnp.concatenate(
            [
                lax.ppermute(tail, axis, [(i, (i + 1) % count) for i in range(ends)]),
                cells,
                lax.ppermute(head, axis, [((i + 1) % count, i) for i in range(ends)]),
            ],
            axis=dim,
        )
    return cells


def from_behind(array, axis, by):
    devices = lax.axis_size(axis)
    pairs = [(i, i + by) for i in range(devices) if 0 <= i + by < devices]
    return lax.ppermute(array, axis, pairs)


def tile_patches(padded, tile_rows, tile_cols):
    shifted = [
        padded[:, row_off : row_off + tile_rows, col_off : col_off + tile_cols].reshape(
            padded.shape[0], tile_rows * tile_cols
        )
        for row_off in range(3)
        for col_off in range(3)
    ]
    return jnp.concatenate(shifted, 0)


def exact_dot(left_mat, right_mat):
    return jnp.dot(
        left_mat, right_mat, precision=lax.Precision.HIGHEST, preferred_element_type=jnp.float32
    )


def flipped(weight_mat):
    channels = weight_mat.shape[0]
    return jnp.transpose(weight_mat.reshape(channels, 9, channels)[:, ::-1, :], (2, 1, 0)).reshape(
        channels, 9 * channels
    )


def local(c_states, c_adjoints, weights):
    group_index = lax.axis_index("layer")
    group_count = lax.axis_size("layer")
    channels, tile_rows, tile_cols = c_states.shape[1:]
    pixels = tile_rows * tile_cols
    depth = weights.shape[0]
    initial_flat = c_states[0].reshape(channels, pixels)
    guess_flat = c_adjoints[0].reshape(channels, pixels)

    def advance(state, weight_mat):
        active = state.astype(jnp.bfloat16).reshape(channels, tile_rows, tile_cols)
        padded = with_halo(active, (("row", 1), ("col", 2)), 1)
        preact = jnp.dot(
            weight_mat,
            tile_patches(padded, tile_rows, tile_cols),
            preferred_element_type=jnp.float32,
        )
        return (state + step_size * jnp.tanh(preact), padded, preact)

    state = initial_flat
    for layer_pos in range(depth):
        state, _, _ = advance(state, weights[layer_pos])
    group_end = state
    summed = jnp.sum(weights[0].astype(jnp.float32).reshape(channels, 9, channels), axis=1)
    coarse_map = jnp.eye(channels, dtype=jnp.float32) + step_size * summed
    is_first = group_index == 0
    is_last = group_index == group_count - 1
    zero_map = jnp.zeros_like(coarse_map)
    blank = jnp.zeros((channels, pixels), jnp.float32)
    fwd_map = jnp.where(is_first, zero_map, coarse_map)
    fwd_offset = jnp.where(is_first, group_end, group_end - exact_dot(coarse_map, initial_flat))

    def state_turn(turn_number, carried):
        return from_behind(exact_dot(fwd_map, carried) + fwd_offset, "layer", 1)

    arrived = lax.fori_loop(0, group_count - 1, state_turn, blank)
    corrected = jnp.where(is_first, initial_flat, arrived)
    state = corrected
    trail = []
    for layer_pos in range(depth):
        state, padded, preact = advance(state, weights[layer_pos])
        trail.append((padded, preact))
    adjoint = guess_flat
    grad_list = [None] * depth
    for layer_pos in reversed(range(depth)):
        padded, preact = trail[layer_pos]
        slope = jnp.tanh(preact)
        source = (adjoint * step_size * (1.0 - slope * slope)).astype(jnp.bfloat16)
        source_pad = with_halo(
            source.reshape(channels, tile_rows, tile_cols), (("row", 1), ("col", 2)), 1
        )
        grad_list[layer_pos] = lax.dot_general(
            source,
            tile_patches(padded, tile_rows, tile_cols),
            (((1,), (1,)), ((), ())),
            preferred_element_type=jnp.float32,
        )
        back = jnp.dot(
            flipped(weights[layer_pos]),
            tile_patches(source_pad, tile_rows, tile_cols),
            preferred_element_type=jnp.float32,
        )
        adjoint = adjoint + back
    weight_grads = lax.psum(jnp.stack(grad_list, 0), ("row", "col"))
    transposed = coarse_map.T
    back_map = jnp.where(is_last, zero_map, transposed)
    back_offset = jnp.where(is_last, adjoint, adjoint - exact_dot(transposed, guess_flat))

    def adjoint_turn(turn_number, carried):
        return from_behind(exact_dot(back_map, carried) + back_offset, "layer", -1)

    returned = lax.fori_loop(0, group_count - 1, adjoint_turn, blank)
    new_adjoint = jnp.where(is_last, guess_flat, returned)
    out_shape = (1, channels, tile_rows, tile_cols)
    return (corrected.reshape(out_shape), new_adjoint.reshape(out_shape), weight_grads)


def solution(mesh):
    placed = (
        P("layer", None, "row", "col"),
        P("layer", None, "row", "col"),
        P("layer", None, None),
    )
    return jax.shard_map(
        local,
        mesh=mesh,
        in_specs=placed,
        out_specs=(
            P("layer", None, "row", "col"),
            P("layer", None, "row", "col"),
            P("layer", None, None),
        ),
        check_vma=False,
    )
```

profile of v0, /device:TPU:1, one launch (start us, length us, event | category | flops | bytes accessed | tf_op | source)
XLA Modules:
  0.0 560.1 jit_solution(8448254401400745606)
XLA Ops:
  8.2 4.5 collective-permute-start.2
  12.8 5.6 collective-permute-start.3
  22.8 4.6 collective-permute-done.4
  27.9 3.7 collective-permute-done.5
  50.3 3.6 collective-permute-done.9
  55.3 3.9 collective-permute-start.10
  61.1 3.3 collective-permute-done.11
  64.7 5.2 collective-permute-start.12
  74.9 4.8 collective-permute-done.13
  81.0 4.5 collective-permute-start.14
  91.1 3.8 collective-permute-start.16
  99.8 3.7 collective-permute-done.17
  105.2 64.2 %while.20 = (s32[]{:T(128)}, f32[64,1024]{1,0:T(8,128)S(1)}, f32[64,64]{1,0:T(8,128)S(1)}, f32[64,1024]{1,0:T(8,128)S(1)}, s32[]{:T(128)}) while((s32[]{:T(128)}, f32[64,1024]{1,0:T(8,128)S(1)}, f32[64,64]{1,0:T(8,128)S(1)}, f32[64,1024]{1,0:T(8,128)S(1)}, s32[]{:T(128)}) %tuple.143), condition=%wide.region_2.3_spmd, body=%wide.region_1.2_spmd.sunk | while | flops 50397184 | bytes 1851493 | solution.py:91
  105.6 4.0 collective-permute-start
  109.6 5.8 %collective-permute-done = f32[64,1024]{1,0:T(8,128)S(1)} collective-permute-done((f32[64,1024]{1,0:T(8,128)S(1)}, f32[64,1024]{1,0:T(8,128)S(1)}, u32[]{:S(2)}, u32[]{:S(2)}) %collective-permute-start) | collective-permute-done | bytes 262176 | tf_op jit(solution)/shard_map/while/body/eval_jaxpr/ppermute | solution.py:29
  115.8 4.0 collective-permute-start
  119.8 5.5 collective-permute-done
  125.7 4.1 collective-permute-start
  129.8 4.5 collective-permute-done
  134.7 5.4 collective-permute-start
  140.1 3.8 collective-permute-done
  144.3 4.1 collective-permute-start
  152.0 5.1 collective-permute-start
  160.8 5.3 collective-permute-start
  169.5 6.1 %collective-permute-start.18 = (bf16[64,1,128]{2,1,0:T(2,128)(2,1)S(1)}, bf16[64,1,128]{2,1,0:T(2,128)(2,1)S(1)}, u32[]{:S(2)}, u32[]{:S(2)}) collective-permute-start(bf16[64,1,128]{2,1,0:T(2,128)(2,1)S(1)} %get-tuple-element.215), channel_id=1, source_target_pairs={{0,8},{8,16},{16,24},{24,32},{32,40},{40,48},{48,56},{1,9},{9,17},... | collective-permute-start | bytes 49160 | tf_op jit(solution)/shard_map/ppermute | solution.py:17
  185.0 3.7 collective-permute-done.20
  189.2 3.6 collective-permute-done.21
  202.2 3.9 collective-permute-start.24
  211.0 4.6 collective-permute-done.25
  217.8 4.2 collective-permute-start.26
  228.2 3.5 collective-permute-start.28
  251.3 3.7 collective-permute-start.32
  260.7 3.8 collective-permute-done.33
  277.7 3.4 collective-permute-start.36
  288.2 6.2 %collective-permute-done.37 = bf16[64,10,1]{2,1,0:T(8,128)(2,1)S(1)} collective-permute-done((bf16[64,10,1]{2,1,0:T(8,128)(2,1)}, bf16[64,10,1]{2,1,0:T(8,128)(2,1)S(1)}, u32[]{:S(2)}, u32[]{:S(2)}) %collective-permute-start.37) | collective-permute-done | bytes 1312 | tf_op jit(solution)/shard_map/ppermute | solution.py:19
  313.3 4.2 collective-permute-done.40
  318.0 4.1 collective-permute-done.41
  340.3 4.1 collective-permute-done.45
  362.3 4.5 collective-permute-done.49
  369.2 71.1 %while.21 = (s32[]{:T(128)}, f32[64,1024]{1,0:T(8,128)S(1)}, f32[64,64]{1,0:T(8,128)S(1)}, f32[64,1024]{1,0:T(8,128)S(1)}, s32[]{:T(128)}) while((s32[]{:T(128)}, f32[64,1024]{1,0:T(8,128)S(1)}, f32[64,64]{1,0:T(8,128)S(1)}, f32[64,1024]{1,0:T(8,128)S(1)}, s32[]{:T(128)}) %tuple.146), condition=%wide.region_4.5_spmd, body=%wide.region_3.4_spmd.sunk | while | flops 50397184 | bytes 1851493 | solution.py:127
  370.9 10.6 %collective-permute-done.1 = f32[64,1024]{1,0:T(8,128)S(1)} collective-permute-done((f32[64,1024]{1,0:T(8,128)S(1)}, f32[64,1024]{1,0:T(8,128)S(1)}, u32[]{:S(2)}, u32[]{:S(2)}) %collective-permute-start.1) | collective-permute-done | bytes 262176 | tf_op jit(solution)/shard_map/while/body/eval_jaxpr/ppermute | solution.py:29
  383.2 10.7 %collective-permute-done.1 = f32[64,1024]{1,0:T(8,128)S(1)} collective-permute-done((f32[64,1024]{1,0:T(8,128)S(1)}, f32[64,1024]{1,0:T(8,128)S(1)}, u32[]{:S(2)}, u32[]{:S(2)}) %collective-permute-start.1) | collective-permute-done | bytes 262176 | tf_op jit(solution)/shard_map/while/body/eval_jaxpr/ppermute | solution.py:29
  395.6 10.1 %collective-permute-done.1 = f32[64,1024]{1,0:T(8,128)S(1)} collective-permute-done((f32[64,1024]{1,0:T(8,128)S(1)}, f32[64,1024]{1,0:T(8,128)S(1)}, u32[]{:S(2)}, u32[]{:S(2)}) %collective-permute-start.1) | collective-permute-done | bytes 262176 | tf_op jit(solution)/shard_map/while/body/eval_jaxpr/ppermute | solution.py:29
  407.3 9.0 %collective-permute-done.1 = f32[64,1024]{1,0:T(8,128)S(1)} collective-permute-done((f32[64,1024]{1,0:T(8,128)S(1)}, f32[64,1024]{1,0:T(8,128)S(1)}, u32[]{:S(2)}, u32[]{:S(2)}) %collective-permute-start.1) | collective-permute-done | bytes 262176 | tf_op jit(solution)/shard_map/while/body/eval_jaxpr/ppermute | solution.py:29
  418.0 6.4 %collective-permute-done.1 = f32[64,1024]{1,0:T(8,128)S(1)} collective-permute-done((f32[64,1024]{1,0:T(8,128)S(1)}, f32[64,1024]{1,0:T(8,128)S(1)}, u32[]{:S(2)}, u32[]{:S(2)}) %collective-permute-start.1) | collective-permute-done | bytes 262176 | tf_op jit(solution)/shard_map/while/body/eval_jaxpr/ppermute | solution.py:29
  426.1 5.8 %collective-permute-done.1 = f32[64,1024]{1,0:T(8,128)S(1)} collective-permute-done((f32[64,1024]{1,0:T(8,128)S(1)}, f32[64,1024]{1,0:T(8,128)S(1)}, u32[]{:S(2)}, u32[]{:S(2)}) %collective-permute-start.1) | collective-permute-done | bytes 262176 | tf_op jit(solution)/shard_map/while/body/eval_jaxpr/ppermute | solution.py:29
  433.5 6.8 %collective-permute-done.1 = f32[64,1024]{1,0:T(8,128)S(1)} collective-permute-done((f32[64,1024]{1,0:T(8,128)S(1)}, f32[64,1024]{1,0:T(8,128)S(1)}, u32[]{:S(2)}, u32[]{:S(2)}) %collective-permute-start.1) | collective-permute-done | bytes 262176 | tf_op jit(solution)/shard_map/while/body/eval_jaxpr/ppermute | solution.py:29
  441.1 110.2 %all-reduce.2.cloned.1.call-done = f32[4,64,576]{2,1,0:T(8,128)} async-done(((f32[4,64,576]{2,1,0:T(8,128)}), f32[4,64,576]{2,1,0:T(8,128)}) %all-reduce.2.cloned.1.call-update) | async-done | bytes 589840 | tf_op jit(solution)/shard_map/psum | solution.py:119
  (376 shorter events, 207.8 us)
Async XLA Ops:
  7.2 544.2 %all-reduce.2.cloned.1.call-start = ((), (), s32[]{:S(2)}) async-start(), calls=%async_computation | async-start | bytes 1310720 | tf_op jit(solution)/shard_map/psum | solution.py:119
  8.2 10.1 %collective-permute-start.2 = (bf16[64,1,128]{2,1,0:T(2,128)(2,1)S(1)}, bf16[64,1,128]{2,1,0:T(2,128)(2,1)S(1)}, u32[]{:S(2)}, u32[]{:S(2)}) collective-permute-start(bf16[64,1,128]{2,1,0:T(2,128)(2,1)S(1)} %get-tuple-element.223), channel_id=1, source_target_pairs={{0,8},{8,16},{16,24},{24,32},{32,40},{40,48},{48,56},{1,9},{9,17},... | collective-permute-start | bytes 49160 | tf_op jit(solution)/shard_map/ppermute | solution.py:17
  12.8 6.4 %collective-permute-start.3 = (bf16[64,1,128]{2,1,0:T(2,128)(2,1)S(1)}, bf16[64,1,128]{2,1,0:T(2,128)(2,1)S(1)}, u32[]{:S(2)}, u32[]{:S(2)}) collective-permute-start(bf16[64,1,128]{2,1,0:T(2,128)(2,1)S(1)} %get-tuple-element.224), channel_id=1, source_target_pairs={{8,0},{16,8},{24,16},{32,24},{40,32},{48,40},{56,48},{9,1},{17,9},... | collective-permute-start | bytes 49160 | tf_op jit(solution)/shard_map/ppermute | solution.py:19
  19.5 7.9 %collective-permute-start.4 = (bf16[64,10,1]{2,1,0:T(8,128)(2,1)S(1)}, bf16[64,10,1]{2,1,0:T(8,128)(2,1)S(1)}, u32[]{:S(2)}, u32[]{:S(2)}) collective-permute-start(bf16[64,10,1]{2,1,0:T(8,128)(2,1)S(1)} %get-tuple-element.176), channel_id=1, source_target_pairs={{0,1},{1,2},{2,3},{3,4},{4,5},{5,6},{6,7},{8,9},{9,10},{10,11},{11... | collective-permute-start | bytes 3848 | tf_op jit(solution)/shard_map/ppermute | solution.py:17
  21.5 10.1 %collective-permute-start.5 = (bf16[64,10,1]{2,1,0:T(8,128)(2,1)S(1)}, bf16[64,10,1]{2,1,0:T(8,128)(2,1)S(1)}, u32[]{:S(2)}, u32[]{:S(2)}) collective-permute-start(bf16[64,10,1]{2,1,0:T(8,128)(2,1)S(1)} %get-tuple-element.175), channel_id=1, source_target_pairs={{1,0},{2,1},{3,2},{4,3},{5,4},{6,5},{7,6},{9,8},{10,9},{11,10},{12... | collective-permute-start | bytes 3848 | tf_op jit(solution)/shard_map/ppermute | solution.py:19
  42.2 7.6 %collective-permute-start.8 = (bf16[64,10,1]{2,1,0:T(8,128)(2,1)S(1)}, bf16[64,10,1]{2,1,0:T(8,128)(2,1)S(1)}, u32[]{:S(2)}, u32[]{:S(2)}) collective-permute-start(bf16[64,10,1]{2,1,0:T(8,128)(2,1)S(1)} %get-tuple-element.174), channel_id=1, source_target_pairs={{0,1},{1,2},{2,3},{3,4},{4,5},{5,6},{6,7},{8,9},{9,10},{10,11},{11... | collective-permute-start | bytes 3848 | tf_op jit(solution)/shard_map/ppermute | solution.py:17
  45.4 8.5 %collective-permute-start.9 = (bf16[64,10,1]{2,1,0:T(8,128)(2,1)S(1)}, bf16[64,10,1]{2,1,0:T(8,128)(2,1)S(1)}, u32[]{:S(2)}, u32[]{:S(2)}) collective-permute-start(bf16[64,10,1]{2,1,0:T(8,128)(2,1)S(1)} %get-tuple-element.173), channel_id=1, source_target_pairs={{1,0},{2,1},{3,2},{4,3},{5,4},{6,5},{7,6},{9,8},{10,9},{11,10},{12... | collective-permute-start | bytes 3848 | tf_op jit(solution)/shard_map/ppermute | solution.py:19
  55.3 5.8 %collective-permute-start.10 = (bf16[64,1,128]{2,1,0:T(2,128)(2,1)S(1)}, bf16[64,1,128]{2,1,0:T(2,128)(2,1)S(1)}, u32[]{:S(2)}, u32[]{:S(2)}) collective-permute-start(bf16[64,1,128]{2,1,0:T(2,128)(2,1)S(1)} %get-tuple-element.219), channel_id=1, source_target_pairs={{0,8},{8,16},{16,24},{24,32},{32,40},{40,48},{48,56},{1,9},{9,17},... | collective-permute-start | bytes 49160 | tf_op jit(solution)/shard_map/ppermute | solution.py:17
  64.7 9.7 %collective-permute-start.12 = (bf16[64,10,1]{2,1,0:T(8,128)(2,1)S(1)}, bf16[64,10,1]{2,1,0:T(8,128)(2,1)S(1)}, u32[]{:S(2)}, u32[]{:S(2)}) collective-permute-start(bf16[64,10,1]{2,1,0:T(8,128)(2,1)S(1)} %get-tuple-element.172), channel_id=1, source_target_pairs={{0,1},{1,2},{2,3},{3,4},{4,5},{5,6},{6,7},{8,9},{9,10},{10,11},{11... | collective-permute-start | bytes 3848 | tf_op jit(solution)/shard_map/ppermute | solution.py:17
  70.8 8.9 %collective-permute-start.13 = (bf16[64,10,1]{2,1,0:T(8,128)(2,1)S(1)}, bf16[64,10,1]{2,1,0:T(8,128)(2,1)S(1)}, u32[]{:S(2)}, u32[]{:S(2)}) collective-permute-start(bf16[64,10,1]{2,1,0:T(8,128)(2,1)S(1)} %get-tuple-element.171), channel_id=1, source_target_pairs={{1,0},{2,1},{3,2},{4,3},{5,4},{6,5},{7,6},{9,8},{10,9},{11,10},{12... | collective-permute-start | bytes 3848 | tf_op jit(solution)/shard_map/ppermute | solution.py:19
  81.0 6.5 %collective-permute-start.14 = (bf16[64,1,128]{2,1,0:T(2,128)(2,1)S(1)}, bf16[64,1,128]{2,1,0:T(2,128)(2,1)S(1)}, u32[]{:S(2)}, u32[]{:S(2)}) collective-permute-start(bf16[64,1,128]{2,1,0:T(2,128)(2,1)S(1)} %get-tuple-element.217), channel_id=1, source_target_pairs={{0,8},{8,16},{16,24},{24,32},{32,40},{40,48},{48,56},{1,9},{9,17},... | collective-permute-start | bytes 49160 | tf_op jit(solution)/shard_map/ppermute | solution.py:17
  91.1 8.2 %collective-permute-start.16 = (bf16[64,10,1]{2,1,0:T(8,128)(2,1)S(1)}, bf16[64,10,1]{2,1,0:T(8,128)(2,1)S(1)}, u32[]{:S(2)}, u32[]{:S(2)}) collective-permute-start(bf16[64,10,1]{2,1,0:T(8,128)(2,1)S(1)} %get-tuple-element.170), channel_id=1, source_target_pairs={{0,1},{1,2},{2,3},{3,4},{4,5},{5,6},{6,7},{8,9},{9,10},{10,11},{11... | collective-permute-start | bytes 3848 | tf_op jit(solution)/shard_map/ppermute | solution.py:17
  95.0 8.5 %collective-permute-start.17 = (bf16[64,10,1]{2,1,0:T(8,128)(2,1)S(1)}, bf16[64,10,1]{2,1,0:T(8,128)(2,1)S(1)}, u32[]{:S(2)}, u32[]{:S(2)}) collective-permute-start(bf16[64,10,1]{2,1,0:T(8,128)(2,1)S(1)} %get-tuple-element.169), channel_id=1, source_target_pairs={{1,0},{2,1},{3,2},{4,3},{5,4},{6,5},{7,6},{9,8},{10,9},{11,10},{12... | collective-permute-start | bytes 3848 | tf_op jit(solution)/shard_map/ppermute | solution.py:19
  105.6 9.8 %collective-permute-start = (f32[64,1024]{1,0:T(8,128)S(1)}, f32[64,1024]{1,0:T(8,128)S(1)}, u32[]{:S(2)}, u32[]{:S(2)}) collective-permute-start(f32[64,1024]{1,0:T(8,128)S(1)} %convolution_add_fusion.4), channel_id=1, source_target_pairs={{0,64},{64,128},{128,192},{192,256},{256,320},{320,384},{384,448},... | collective-permute-start | bytes 786440 | tf_op jit(solution)/shard_map/while/body/eval_jaxpr/ppermute | solution.py:29
  115.8 9.5 %collective-permute-start = (f32[64,1024]{1,0:T(8,128)S(1)}, f32[64,1024]{1,0:T(8,128)S(1)}, u32[]{:S(2)}, u32[]{:S(2)}) collective-permute-start(f32[64,1024]{1,0:T(8,128)S(1)} %convolution_add_fusion.4), channel_id=1, source_target_pairs={{0,64},{64,128},{128,192},{192,256},{256,320},{320,384},{384,448},... | collective-permute-start | bytes 786440 | tf_op jit(solution)/shard_map/while/body/eval_jaxpr/ppermute | solution.py:29
  125.7 8.7 %collective-permute-start = (f32[64,1024]{1,0:T(8,128)S(1)}, f32[64,1024]{1,0:T(8,128)S(1)}, u32[]{:S(2)}, u32[]{:S(2)}) collective-permute-start(f32[64,1024]{1,0:T(8,128)S(1)} %convolution_add_fusion.4), channel_id=1, source_target_pairs={{0,64},{64,128},{128,192},{192,256},{256,320},{320,384},{384,448},... | collective-permute-start | bytes 786440 | tf_op jit(solution)/shard_map/while/body/eval_jaxpr/ppermute | solution.py:29
  134.7 9.2 %collective-permute-start = (f32[64,1024]{1,0:T(8,128)S(1)}, f32[64,1024]{1,0:T(8,128)S(1)}, u32[]{:S(2)}, u32[]{:S(2)}) collective-permute-start(f32[64,1024]{1,0:T(8,128)S(1)} %convolution_add_fusion.4), channel_id=1, source_target_pairs={{0,64},{64,128},{128,192},{192,256},{256,320},{320,384},{384,448},... | collective-permute-start | bytes 786440 | tf_op jit(solution)/shard_map/while/body/eval_jaxpr/ppermute | solution.py:29
  144.3 7.4 %collective-permute-start = (f32[64,1024]{1,0:T(8,128)S(1)}, f32[64,1024]{1,0:T(8,128)S(1)}, u32[]{:S(2)}, u32[]{:S(2)}) collective-permute-start(f32[64,1024]{1,0:T(8,128)S(1)} %convolution_add_fusion.4), channel_id=1, source_target_pairs={{0,64},{64,128},{128,192},{192,256},{256,320},{320,384},{384,448},... | collective-permute-start | bytes 786440 | tf_op jit(solution)/shard_map/while/body/eval_jaxpr/ppermute | solution.py:29
  152.0 8.3 %collective-permute-start = (f32[64,1024]{1,0:T(8,128)S(1)}, f32[64,1024]{1,0:T(8,128)S(1)}, u32[]{:S(2)}, u32[]{:S(2)}) collective-permute-start(f32[64,1024]{1,0:T(8,128)S(1)} %convolution_add_fusion.4), channel_id=1, source_target_pairs={{0,64},{64,128},{128,192},{192,256},{256,320},{320,384},{384,448},... | collective-permute-start | bytes 786440 | tf_op jit(solution)/shard_map/while/body/eval_jaxpr/ppermute | solution.py:29
  160.8 8.6 %collective-permute-start = (f32[64,1024]{1,0:T(8,128)S(1)}, f32[64,1024]{1,0:T(8,128)S(1)}, u32[]{:S(2)}, u32[]{:S(2)}) collective-permute-start(f32[64,1024]{1,0:T(8,128)S(1)} %convolution_add_fusion.4), channel_id=1, source_target_pairs={{0,64},{64,128},{128,192},{192,256},{256,320},{320,384},{384,448},... | collective-permute-start | bytes 786440 | tf_op jit(solution)/shard_map/while/body/eval_jaxpr/ppermute | solution.py:29
  169.5 9.0 %collective-permute-start.18 = (bf16[64,1,128]{2,1,0:T(2,128)(2,1)S(1)}, bf16[64,1,128]{2,1,0:T(2,128)(2,1)S(1)}, u32[]{:S(2)}, u32[]{:S(2)}) collective-permute-start(bf16[64,1,128]{2,1,0:T(2,128)(2,1)S(1)} %get-tuple-element.215), channel_id=1, source_target_pairs={{0,8},{8,16},{16,24},{24,32},{32,40},{40,48},{48,56},{1,9},{9,17},... | collective-permute-start | bytes 49160 | tf_op jit(solution)/shard_map/ppermute | solution.py:17
  181.1 7.6 %collective-permute-start.20 = (bf16[64,10,1]{2,1,0:T(8,128)(2,1)S(1)}, bf16[64,10,1]{2,1,0:T(8,128)(2,1)S(1)}, u32[]{:S(2)}, u32[]{:S(2)}) collective-permute-start(bf16[64,10,1]{2,1,0:T(8,128)(2,1)S(1)} %get-tuple-element.168), channel_id=1, source_target_pairs={{0,1},{1,2},{2,3},{3,4},{4,5},{5,6},{6,7},{8,9},{9,10},{10,11},{11... | collective-permute-start | bytes 3848 | tf_op jit(solution)/shard_map/ppermute | solution.py:17
  183.5 9.3 %collective-permute-start.21 = (bf16[64,10,1]{2,1,0:T(8,128)(2,1)S(1)}, bf16[64,10,1]{2,1,0:T(8,128)(2,1)S(1)}, u32[]{:S(2)}, u32[]{:S(2)}) collective-permute-start(bf16[64,10,1]{2,1,0:T(8,128)(2,1)S(1)} %get-tuple-element.167), channel_id=1, source_target_pairs={{1,0},{2,1},{3,2},{4,3},{5,4},{6,5},{7,6},{9,8},{10,9},{11,10},{12... | collective-permute-start | bytes 3848 | tf_op jit(solution)/shard_map/ppermute | solution.py:19
  202.2 8.3 %collective-permute-start.24 = (bf16[64,10,1]{2,1,0:T(8,128)(2,1)S(1)}, bf16[64,10,1]{2,1,0:T(8,128)(2,1)S(1)}, u32[]{:S(2)}, u32[]{:S(2)}) collective-permute-start(bf16[64,10,1]{2,1,0:T(8,128)(2,1)S(1)} %get-tuple-element.166), channel_id=1, source_target_pairs={{0,1},{1,2},{2,3},{3,4},{4,5},{5,6},{6,7},{8,9},{9,10},{10,11},{11... | collective-permute-start | bytes 3848 | tf_op jit(solution)/shard_map/ppermute | solution.py:17
  206.1 9.6 %collective-permute-start.25 = (bf16[64,10,1]{2,1,0:T(8,128)(2,1)S(1)}, bf16[64,10,1]{2,1,0:T(8,128)(2,1)S(1)}, u32[]{:S(2)}, u32[]{:S(2)}) collective-permute-start(bf16[64,10,1]{2,1,0:T(8,128)(2,1)S(1)} %get-tuple-element.165), channel_id=1, source_target_pairs={{1,0},{2,1},{3,2},{4,3},{5,4},{6,5},{7,6},{9,8},{10,9},{11,10},{12... | collective-permute-start | bytes 3848 | tf_op jit(solution)/shard_map/ppermute | solution.py:19
  217.8 6.1 %collective-permute-start.26 = (bf16[64,1,128]{2,1,0:T(2,128)(2,1)S(1)}, bf16[64,1,128]{2,1,0:T(2,128)(2,1)S(1)}, u32[]{:S(2)}, u32[]{:S(2)}) collective-permute-start(bf16[64,1,128]{2,1,0:T(2,128)(2,1)S(1)} %get-tuple-element.211), channel_id=1, source_target_pairs={{0,8},{8,16},{16,24},{24,32},{32,40},{40,48},{48,56},{1,9},{9,17},... | collective-permute-start | bytes 49160 | tf_op jit(solution)/shard_map/ppermute | solution.py:17
  228.2 7.6 %collective-permute-start.28 = (bf16[64,10,1]{2,1,0:T(8,128)(2,1)}, bf16[64,10,1]{2,1,0:T(8,128)(2,1)}, u32[]{:S(2)}, u32[]{:S(2)}) collective-permute-start(bf16[64,10,1]{2,1,0:T(8,128)(2,1)} %get-tuple-element.164), channel_id=1, source_target_pairs={{0,1},{1,2},{2,3},{3,4},{4,5},{5,6},{6,7},{8,9},{9,10},{10,11},{11... | collective-permute-start | bytes 3848 | tf_op jit(solution)/shard_map/ppermute | solution.py:17
  231.7 8.7 %collective-permute-start.29 = (bf16[64,10,1]{2,1,0:T(8,128)(2,1)}, bf16[64,10,1]{2,1,0:T(8,128)(2,1)S(1)}, u32[]{:S(2)}, u32[]{:S(2)}) collective-permute-start(bf16[64,10,1]{2,1,0:T(8,128)(2,1)} %get-tuple-element.163), channel_id=1, source_target_pairs={{1,0},{2,1},{3,2},{4,3},{5,4},{6,5},{7,6},{9,8},{10,9},{11,10},{12... | collective-permute-start | bytes 3848 | tf_op jit(solution)/shard_map/ppermute | solution.py:19
  251.3 7.7 %collective-permute-start.32 = (bf16[64,10,1]{2,1,0:T(8,128)(2,1)}, bf16[64,10,1]{2,1,0:T(8,128)(2,1)}, u32[]{:S(2)}, u32[]{:S(2)}) collective-permute-start(bf16[64,10,1]{2,1,0:T(8,128)(2,1)} %get-tuple-element.162), channel_id=1, source_target_pairs={{0,1},{1,2},{2,3},{3,4},{4,5},{5,6},{6,7},{8,9},{9,10},{10,11},{11... | collective-permute-start | bytes 3848 | tf_op jit(solution)/shard_map/ppermute | solution.py:17
  255.7 8.7 %collective-permute-start.33 = (bf16[64,10,1]{2,1,0:T(8,128)(2,1)}, bf16[64,10,1]{2,1,0:T(8,128)(2,1)S(1)}, u32[]{:S(2)}, u32[]{:S(2)}) collective-permute-start(bf16[64,10,1]{2,1,0:T(8,128)(2,1)} %get-tuple-element.161), channel_id=1, source_target_pairs={{1,0},{2,1},{3,2},{4,3},{5,4},{6,5},{7,6},{9,8},{10,9},{11,10},{12... | collective-permute-start | bytes 3848 | tf_op jit(solution)/shard_map/ppermute | solution.py:19
  268.5 6.0 %collective-permute-start.34 = (bf16[64,1,128]{2,1,0:T(2,128)(2,1)}, bf16[64,1,128]{2,1,0:T(2,128)(2,1)S(1)}, u32[]{:S(2)}, u32[]{:S(2)}) collective-permute-start(bf16[64,1,128]{2,1,0:T(2,128)(2,1)} %get-tuple-element.207), channel_id=1, source_target_pairs={{0,8},{8,16},{16,24},{24,32},{32,40},{40,48},{48,56},{1,9},{9,17},... | collective-permute-start | bytes 49160 | tf_op jit(solution)/shard_map/ppermute | solution.py:17
  277.7 8.7 %collective-permute-start.36 = (bf16[64,10,1]{2,1,0:T(8,128)(2,1)}, bf16[64,10,1]{2,1,0:T(8,128)(2,1)}, u32[]{:S(2)}, u32[]{:S(2)}) collective-permute-start(bf16[64,10,1]{2,1,0:T(8,128)(2,1)} %get-tuple-element.160), channel_id=1, source_target_pairs={{0,1},{1,2},{2,3},{3,4},{4,5},{5,6},{6,7},{8,9},{9,10},{10,11},{11... | collective-permute-start | bytes 3848 | tf_op jit(solution)/shard_map/ppermute | solution.py:17
  285.2 9.3 %collective-permute-start.37 = (bf16[64,10,1]{2,1,0:T(8,128)(2,1)}, bf16[64,10,1]{2,1,0:T(8,128)(2,1)S(1)}, u32[]{:S(2)}, u32[]{:S(2)}) collective-permute-start(bf16[64,10,1]{2,1,0:T(8,128)(2,1)} %get-tuple-element.159), channel_id=1, source_target_pairs={{1,0},{2,1},{3,2},{4,3},{5,4},{6,5},{7,6},{9,8},{10,9},{11,10},{12... | collective-permute-start | bytes 3848 | tf_op jit(solution)/shard_map/ppermute | solution.py:19
  298.8 9.9 %collective-permute-start.38 = (bf16[64,1,128]{2,1,0:T(2,128)(2,1)}, bf16[64,1,128]{2,1,0:T(2,128)(2,1)S(1)}, u32[]{:S(2)}, u32[]{:S(2)}) collective-permute-start(bf16[64,1,128]{2,1,0:T(2,128)(2,1)} %get-tuple-element.205), channel_id=1, source_target_pairs={{0,8},{8,16},{16,24},{24,32},{32,40},{40,48},{48,56},{1,9},{9,17},... | collective-permute-start | bytes 49160 | tf_op jit(solution)/shard_map/ppermute | solution.py:17
  300.7 8.0 %collective-permute-start.39 = (bf16[64,1,128]{2,1,0:T(2,128)(2,1)}, bf16[64,1,128]{2,1,0:T(2,128)(2,1)S(1)}, u32[]{:S(2)}, u32[]{:S(2)}) collective-permute-start(bf16[64,1,128]{2,1,0:T(2,128)(2,1)} %get-tuple-element.206), channel_id=1, source_target_pairs={{8,0},{16,8},{24,16},{32,24},{40,32},{48,40},{56,48},{9,1},{17,9},... | collective-permute-start | bytes 49160 | tf_op jit(solution)/shard_map/ppermute | solution.py:19
  309.0 8.4 %collective-permute-start.40 = (bf16[64,10,1]{2,1,0:T(8,128)(2,1)S(1)}, bf16[64,10,1]{2,1,0:T(8,128)(2,1)S(1)}, u32[]{:S(2)}, u32[]{:S(2)}) collective-permute-start(bf16[64,10,1]{2,1,0:T(8,128)(2,1)S(1)} %get-tuple-element.158), channel_id=1, source_target_pairs={{0,1},{1,2},{2,3},{3,4},{4,5},{5,6},{6,7},{8,9},{9,10},{10,11},{11... | collective-permute-start | bytes 3848 | tf_op jit(solution)/shard_map/ppermute | solution.py:17
  312.0 10.1 %collective-permute-start.41 = (bf16[64,10,1]{2,1,0:T(8,128)(2,1)S(1)}, bf16[64,10,1]{2,1,0:T(8,128)(2,1)S(1)}, u32[]{:S(2)}, u32[]{:S(2)}) collective-permute-start(bf16[64,10,1]{2,1,0:T(8,128)(2,1)S(1)} %get-tuple-element.157), channel_id=1, source_target_pairs={{1,0},{2,1},{3,2},{4,3},{5,4},{6,5},{7,6},{9,8},{10,9},{11,10},{12... | collective-permute-start | bytes 3848 | tf_op jit(solution)/shard_map/ppermute | solution.py:19
  331.8 8.0 %collective-permute-start.44 = (bf16[64,10,1]{2,1,0:T(8,128)(2,1)S(1)}, bf16[64,10,1]{2,1,0:T(8,128)(2,1)S(1)}, u32[]{:S(2)}, u32[]{:S(2)}) collective-permute-start(bf16[64,10,1]{2,1,0:T(8,128)(2,1)S(1)} %get-tuple-element.156), channel_id=1, source_target_pairs={{0,1},{1,2},{2,3},{3,4},{4,5},{5,6},{6,7},{8,9},{9,10},{10,11},{11... | collective-permute-start | bytes 3848 | tf_op jit(solution)/shard_map/ppermute | solution.py:17
  335.4 9.0 %collective-permute-start.45 = (bf16[64,10,1]{2,1,0:T(8,128)(2,1)S(1)}, bf16[64,10,1]{2,1,0:T(8,128)(2,1)S(1)}, u32[]{:S(2)}, u32[]{:S(2)}) collective-permute-start(bf16[64,10,1]{2,1,0:T(8,128)(2,1)S(1)} %get-tuple-element.155), channel_id=1, source_target_pairs={{1,0},{2,1},{3,2},{4,3},{5,4},{6,5},{7,6},{9,8},{10,9},{11,10},{12... | collective-permute-start | bytes 3848 | tf_op jit(solution)/shard_map/ppermute | solution.py:19
  354.0 7.8 %collective-permute-start.48 = (bf16[64,10,1]{2,1,0:T(8,128)(2,1)S(1)}, bf16[64,10,1]{2,1,0:T(8,128)(2,1)S(1)}, u32[]{:S(2)}, u32[]{:S(2)}) collective-permute-start(bf16[64,10,1]{2,1,0:T(8,128)(2,1)S(1)} %get-tuple-element.154), channel_id=1, source_target_pairs={{0,1},{1,2},{2,3},{3,4},{4,5},{5,6},{6,7},{8,9},{9,10},{10,11},{11... | collective-permute-start | bytes 3848 | tf_op jit(solution)/shard_map/ppermute | solution.py:17
  357.8 9.0 %collective-permute-start.49 = (bf16[64,10,1]{2,1,0:T(8,128)(2,1)S(1)}, bf16[64,10,1]{2,1,0:T(8,128)(2,1)S(1)}, u32[]{:S(2)}, u32[]{:S(2)}) collective-permute-start(bf16[64,10,1]{2,1,0:T(8,128)(2,1)S(1)} %get-tuple-element.153), channel_id=1, source_target_pairs={{1,0},{2,1},{3,2},{4,3},{5,4},{6,5},{7,6},{9,8},{10,9},{11,10},{12... | collective-permute-start | bytes 3848 | tf_op jit(solution)/shard_map/ppermute | solution.py:19
  369.6 11.9 %collective-permute-start.1 = (f32[64,1024]{1,0:T(8,128)S(1)}, f32[64,1024]{1,0:T(8,128)S(1)}, u32[]{:S(2)}, u32[]{:S(2)}) collective-permute-start(f32[64,1024]{1,0:T(8,128)S(1)} %convolution_add_fusion.5), channel_id=1, source_target_pairs={{64,0},{128,64},{192,128},{256,192},{320,256},{384,320},{448,384},... | collective-permute-start | bytes 786440 | tf_op jit(solution)/shard_map/while/body/eval_jaxpr/ppermute | solution.py:29
  381.9 12.0 %collective-permute-start.1 = (f32[64,1024]{1,0:T(8,128)S(1)}, f32[64,1024]{1,0:T(8,128)S(1)}, u32[]{:S(2)}, u32[]{:S(2)}) collective-permute-start(f32[64,1024]{1,0:T(8,128)S(1)} %convolution_add_fusion.5), channel_id=1, source_target_pairs={{64,0},{128,64},{192,128},{256,192},{320,256},{384,320},{448,384},... | collective-permute-start | bytes 786440 | tf_op jit(solution)/shard_map/while/body/eval_jaxpr/ppermute | solution.py:29
  394.3 11.4 %collective-permute-start.1 = (f32[64,1024]{1,0:T(8,128)S(1)}, f32[64,1024]{1,0:T(8,128)S(1)}, u32[]{:S(2)}, u32[]{:S(2)}) collective-permute-start(f32[64,1024]{1,0:T(8,128)S(1)} %convolution_add_fusion.5), channel_id=1, source_target_pairs={{64,0},{128,64},{192,128},{256,192},{320,256},{384,320},{448,384},... | collective-permute-start | bytes 786440 | tf_op jit(solution)/shard_map/while/body/eval_jaxpr/ppermute | solution.py:29
  406.0 10.3 %collective-permute-start.1 = (f32[64,1024]{1,0:T(8,128)S(1)}, f32[64,1024]{1,0:T(8,128)S(1)}, u32[]{:S(2)}, u32[]{:S(2)}) collective-permute-start(f32[64,1024]{1,0:T(8,128)S(1)} %convolution_add_fusion.5), channel_id=1, source_target_pairs={{64,0},{128,64},{192,128},{256,192},{320,256},{384,320},{448,384},... | collective-permute-start | bytes 786440 | tf_op jit(solution)/shard_map/while/body/eval_jaxpr/ppermute | solution.py:29
  416.7 7.7 %collective-permute-start.1 = (f32[64,1024]{1,0:T(8,128)S(1)}, f32[64,1024]{1,0:T(8,128)S(1)}, u32[]{:S(2)}, u32[]{:S(2)}) collective-permute-start(f32[64,1024]{1,0:T(8,128)S(1)} %convolution_add_fusion.5), channel_id=1, source_target_pairs={{64,0},{128,64},{192,128},{256,192},{320,256},{384,320},{448,384},... | collective-permute-start | bytes 786440 | tf_op jit(solution)/shard_map/while/body/eval_jaxpr/ppermute | solution.py:29
  424.8 7.1 %collective-permute-start.1 = (f32[64,1024]{1,0:T(8,128)S(1)}, f32[64,1024]{1,0:T(8,128)S(1)}, u32[]{:S(2)}, u32[]{:S(2)}) collective-permute-start(f32[64,1024]{1,0:T(8,128)S(1)} %convolution_add_fusion.5), channel_id=1, source_target_pairs={{64,0},{128,64},{192,128},{256,192},{320,256},{384,320},{448,384},... | collective-permute-start | bytes 786440 | tf_op jit(solution)/shard_map/while/body/eval_jaxpr/ppermute | solution.py:29
  432.2 8.1 %collective-permute-start.1 = (f32[64,1024]{1,0:T(8,128)S(1)}, f32[64,1024]{1,0:T(8,128)S(1)}, u32[]{:S(2)}, u32[]{:S(2)}) collective-permute-start(f32[64,1024]{1,0:T(8,128)S(1)} %convolution_add_fusion.5), channel_id=1, source_target_pairs={{64,0},{128,64},{192,128},{256,192},{320,256},{384,320},{448,384},... | collective-permute-start | bytes 786440 | tf_op jit(solution)/shard_map/while/body/eval_jaxpr/ppermute | solution.py:29
  (42 other events, 237.3 us)
Sparse Core Ops, SparseCore 0:
  357.9 193.3 all-reduce.1
where the time goes:
time: 563 us; the launch traced here: 560 us
  waiting for transfers between devices  312 us (55%)
  starting transfers between devices  164 us (29%)
  local copies, waits for them, and re-layouts  28.5 us (5%)
  other arithmetic  24.9 us (4%)
  between operations  16.1 us (3%)
  matrix products  13.7 us (2%)
    psum x1, waiting for transfers between devices, local(): weight_grads = lax.psum(jnp.stack(grad_list, 0), ('row', 'col'))  110 us
    ppermute x14, waiting for transfers between devices, from_behind(): return lax.ppermute(array, axis, pairs)  88.8 us
    ppermute x24, waiting for transfers between devices, with_halo(): lax.ppermute(head, axis, [((i + 1) % count, i) for i in range(ends)])  78.5 us
    ppermute x24, starting transfers between devices, with_halo(): lax.ppermute(tail, axis, [(i, (i + 1) % count) for i in range(ends)])  77.9 us
    ppermute x24, starting transfers between devices, with_halo(): lax.ppermute(head, axis, [((i + 1) % count, i) for i in range(ends)])  45.4 us
    ppermute x14, starting transfers between devices, from_behind(): return lax.ppermute(array, axis, pairs)  41.1 us
    ppermute x24, waiting for transfers between devices, with_halo(): lax.ppermute(tail, axis, [(i, (i + 1) % count) for i in range(ends)])  34.7 us
    concatenate x36, other arithmetic, with_halo(): jnp.concatenate([lax.ppermute(tail, axis, [(i, (i + 1) % count) for i in...  21.9 us
  transfers between devices with their start and end apart: 63, of which 49 were waited for; matrix products, arithmetic and copies ran while one was open for 5% of the time, Pallas kernels for 0%

commit v1 on v0

v1 whole, which is shorter than its diff:
```python
import functools

import jax
import jax.numpy as jnp
from jax import lax
from jax.experimental import pallas as pl
from jax.experimental.pallas import tpu as pltpu
from jax.sharding import PartitionSpec as P

MESH = pl.DeviceIdType.MESH
F32 = jnp.float32
BF16 = jnp.bfloat16

CH = 64
LG = 4
TR = 8
TC = 128
NP = 8
HALO = 8
ST = TC + 2 * HALO
RW = TR + 2 * HALO
LEN = RW * ST
PAD = 256
WIDE = LEN + 2 * PAD
NEAR = ((0, -1), (0, 1), (-1, -1), (-1, 1), (1, -1), (1, 1))
PIECE = 144
step_size = 0.2


def span(halo):
    low, high = (HALO - halo) * ST, (HALO + TR + halo) * ST
    return low // 128 * 128, -(-high // 128) * 128


def chunks(bounds, size=256):
    low, high = bounds
    return [(at, min(size, high - at)) for at in range(low, high, size)]


def shifted(ref, rows, start, size):
    begin = start + PAD
    low = begin // 128 * 128
    off = begin - low
    if off == 0:
        return ref[rows, low : low + size]
    width = size + 128
    window = ref[rows, low : low + width]
    return pltpu.roll(window, width - off, 1)[:, :size]


def split3(matrix):
    high = matrix.astype(BF16)
    low = (matrix - high.astype(F32)).astype(BF16)
    return high, low


def body(
    x_in, q_in, w_ref, wall_ref, wback_ref,
    ns_ref, na_ref, wg_ref,
    x0, q0, n0, main_x, pack_x, main_q, pack_q, main_n, pack_n,
    rm_x, rp_x, rm_q, rp_q, rm_n, rp_n,
    amap, atmap, ga, gat, gc, gq, fb, gf, db, rd, dl, rl, gb, gg, eb, re,
    inside, own, xw, qw, yw, sa, ts, ss, so, sw,
    gpf, gpb, rr, hb, rc, pb, gall,
    send, recv,
):
    layer, row, col = (lax.axis_index(name) for name in ("layer", "row", "col"))
    finish = []
    counter = [0, 0]

    def slots(kind, count):
        first = counter[kind]
        counter[kind] += count
        return first

    def at(which, axis_name, by):
        return {axis_name: lax.rem(which + by + NP, NP)}

    def push(src, dst, send_at, recv_at, device):
        copy = pltpu.make_async_remote_copy(
            src_ref=src, dst_ref=dst, send_sem=send.at[send_at], recv_sem=recv.at[recv_at],
            device_id=device, device_id_type=MESH,
        )
        copy.start()
        return copy

    def arrived(dst, recv_at):
        pltpu.make_async_remote_copy(
            src_ref=dst, dst_ref=dst, send_sem=send.at[0], recv_sem=recv.at[recv_at],
            device_id={"layer": layer}, device_id_type=MESH,
        ).wait_recv()

    barrier = pltpu.get_barrier_semaphore()
    for by in range(1, NP):
        for which, name in ((layer, "layer"), (row, "row"), (col, "col")):
            pl.semaphore_signal(barrier, inc=1, device_id=at(which, name, by), device_id_type=MESH)
    for down, right in NEAR[2:]:
        pl.semaphore_signal(
            barrier, inc=1, device_id=at(row, "row", down) | at(col, "col", right), device_id_type=MESH
        )

    spot = lax.broadcasted_iota(jnp.int32, (TR * TC, 128), 0)
    lane = lax.broadcasted_iota(jnp.int32, (TR * TC, 128), 1)
    column, line = spot % TC, spot // TC
    picks = (lane < 64) & (column < HALO) & (lane == line * HALO + column)
    picks |= (lane >= 64) & (column >= TC - HALO) & (lane - 64 == line * HALO + column - (TC - HALO))
    edges = picks.astype(F32).astype(BF16)

    def pack_edges(main, pack):
        pack[...] = jnp.dot(main[...], edges, preferred_element_type=F32).astype(BF16)

    for r in range(TR):
        value = x_in[0, :, r, :]
        x0[r] = value
        main_x[:, r * TC : (r + 1) * TC] = value.astype(BF16)
    pack_edges(main_x, pack_x)

    def send_halo(main, pack, rows, rm, rp):
        first_s, first_r = slots(0, 8), slots(1, 8)
        width = rows * TC
        top, bottom = main.at[:, pl.ds(0, width)], main.at[:, pl.ds((TR - rows) * TC, width)]
        finish.append(push(
            bottom, rm.at[0, :, pl.ds((TR - rows) * TC, width)], first_s, first_r, at(row, "row", 1)
        ))
        finish.append(push(top, rm.at[1, :, pl.ds(0, width)], first_s + 1, first_r + 1, at(row, "row", -1)))
        for number, (down, right) in enumerate(NEAR):
            there = NEAR.index((-down, -right))
            device = at(col, "col", right)
            if down:
                device = device | at(row, "row", down)
            finish.append(push(pack, rp.at[there], first_s + 2 + number, first_r + 2 + there, device))

        def wait():
            arrived(rm.at[0, :, pl.ds((TR - rows) * TC, width)], first_r)
            arrived(rm.at[1, :, pl.ds(0, width)], first_r + 1)
            for number in range(6):
                arrived(rp.at[number], first_r + 2 + number)

        return wait

    def to_all(which, name, src_of, dst, dynamic=True):
        first_s, first_r = slots(0, NP), slots(1, NP)
        for by in range(1, NP):
            peer = lax.rem(which + by, NP)
            finish.append(push(
                src_of(peer), dst.at[which], first_s + by, first_r + which, {name: peer}
            ))

        def wait():
            for by in range(1, NP):
                peer = lax.rem(which + by, NP)
                arrived(dst.at[peer], first_r + peer)

        return wait

    pl.semaphore_wait(barrier, 3 * (NP - 1) + 4)
    wait_x = send_halo(main_x, pack_x, 4, rm_x, rp_x)

    tap_row = lax.broadcasted_iota(jnp.int32, (9 * CH, CH), 0)
    tap_col = lax.broadcasted_iota(jnp.int32, (9 * CH, CH), 1)
    fold = (tap_row % CH == tap_col).astype(F32).astype(BF16)
    fold_t = (
        lax.broadcasted_iota(jnp.int32, (CH, 9 * CH), 1) % CH == lax.broadcasted_iota(jnp.int32, (CH, 9 * CH), 0)
    ).astype(F32).astype(BF16)
    eye = (
        lax.broadcasted_iota(jnp.int32, (CH, CH), 0) == lax.broadcasted_iota(jnp.int32, (CH, CH), 1)
    ).astype(F32)
    summed = jnp.dot(w_ref[0], fold, preferred_element_type=F32)
    summed_t = lax.dot_general(fold_t, w_ref[0], (((1,), (1,)), ((), ())), preferred_element_type=F32)
    amap[...] = jnp.concatenate(split3(eye + step_size * summed), axis=1)
    atmap[...] = jnp.concatenate(split3(eye + step_size * summed_t), axis=1)
    wait_a = to_all(layer, "layer", lambda peer: amap, ga)
    wait_c = to_all(layer, "layer", lambda peer: x0.at[peer], gc)
    ga[layer] = amap[...]
    gat[layer] = atmap[...]
    gc[layer] = x0[layer]

    for r in range(TR):
        value = q_in[0, :, r, :]
        q0[r] = value
        main_q[:, r * TC : (r + 1) * TC] = value.astype(BF16)
    pack_edges(main_q, pack_q)
    wait_q = send_halo(main_q, pack_q, 4, rm_q, rp_q)

    place = lax.broadcasted_iota(jnp.int32, (8, WIDE), 1)
    lanes = place - PAD
    held = (lanes >= 0) & (lanes < LEN)
    safe = jnp.where(held, lanes, 0)
    r_at, c_at = safe // ST - HALO, safe % ST - HALO
    r_all, c_all = row * TR + r_at, col * TC + c_at
    ok = held & (r_all >= 0) & (r_all < NP * TR) & (c_all >= 0) & (c_all < NP * TC)
    inside[...] = ok.astype(F32)
    mine = held & (r_at >= 0) & (r_at < TR) & (c_at >= 0) & (c_at < TC)
    own[...] = mine.astype(F32)
    for ref in (xw, qw):
        ref[...] = jnp.zeros_like(ref)
    yw[...] = jnp.zeros_like(yw)
    so[...] = jnp.zeros_like(so)

    def assemble(ref, tile, rm, rp, halo):
        sides = ((rp[2], rp[3]), (rp[0], rp[1]), (rp[4], rp[5]))
        for line in range(HALO - halo, HALO + TR + halo):
            block, r = line // TR, line % TR
            start = PAD + line * ST
            if block == 1:
                main = tile[r]
            else:
                main = rm[block // 2, :, r * TC : (r + 1) * TC].astype(F32)
            left, right = sides[block]
            ref[:, start : start + ST] = jnp.concatenate(
                [
                    left[:, 64 + r * HALO : 64 + (r + 1) * HALO].astype(F32),
                    main,
                    right[:, r * HALO : (r + 1) * HALO].astype(F32),
                ],
                axis=1,
            )

    def spread(take, dst, bounds):
        for start, size in chunks(bounds):
            window = take(start - 128, size + 256)
            width = size + 256
            dst[0:CH, start : start + size] = pltpu.roll(window, 1, 1)[:, 128 : 128 + size].astype(BF16)
            dst[CH : 2 * CH, start : start + size] = window[:, 128 : 128 + size].astype(BF16)
            dst[2 * CH : 3 * CH, start : start + size] = pltpu.roll(window, width - 1, 1)[
                :, 128 : 128 + size
            ].astype(BF16)

    def multiply(matrix, src, bounds):
        for start, size in chunks(bounds):
            yw[:, PAD + start : PAD + start + size] = jnp.dot(
                matrix, src[:, start : start + size], preferred_element_type=F32
            )

    def gathered(start, size):
        total = yw[CH : 2 * CH, PAD + start : PAD + start + size]
        total += shifted(yw, slice(0, CH), start - ST, size)
        return total + shifted(yw, slice(2 * CH, 3 * CH), start + ST, size)

    def window_of(ref, start, size):
        return ref[:, PAD + start : PAD + start + size]

    def masked_state(start, size):
        return window_of(xw, start, size) * window_of(inside, start, size)[0:1]

    def forward(number, cols, slopes, halo):
        spread(masked_state, cols, span(halo + 1))
        multiply(wall_ref[number], cols, span(halo + 1))
        for start, size in chunks(span(halo)):
            bent = jnp.tanh(gathered(start, size))
            xw[:, PAD + start : PAD + start + size] += step_size * bent
            if slopes is not None:
                slopes[:, PAD + start : PAD + start + size] = step_size * (1.0 - bent * bent)

    def tile_row(ref, r):
        return shifted(ref, slice(0, CH), (HALO + r) * ST + HALO, TC)

    wait_x()
    assemble(xw, x0, rm_x, rp_x, 4)
    for number in range(LG):
        forward(number, sa.at[0], None, LG - 1 - number)
    for r in range(TR):
        fb[r] = (tile_row(xw, r) - x0[r]).astype(BF16)
    wait_f = to_all(layer, "layer", lambda peer: fb.at[peer], gf)
    gf[layer] = fb[layer]
    wait_a()
    wait_c()
    wait_f()

    def sweep(first, last, by, moves, guesses, maps, out, land, rest=None, rest_land=None):
        first_s, first_r = slots(0, NP), slots(1, NP)
        rest_s, rest_r = slots(0, NP), slots(1, NP)

        def hand(k, src, dst, s_at, r_at):
            @pl.when(layer != k)
            def _():
                push(src.at[k], dst.at[layer], s_at + k, r_at + layer, {"layer": k})

            @pl.when(layer == k)
            def _():
                dst[layer] = src[k]

        offset = None
        for k in range(first, last, by):
            change = moves[k].astype(F32) + (guesses[k] - guesses[k + by])
            if offset is not None:
                high, low = split3(offset)
                wide = maps[k]
                change += jnp.dot(
                    jnp.concatenate([wide, wide[:, :CH]], axis=1),
                    jnp.concatenate([high, high, low], axis=0),
                    preferred_element_type=F32,
                )
            offset = change
            high, low = split3(guesses[k + by] + offset)
            out[k + by] = high
            if rest is not None:
                rest[k + by] = low
            hand(k + by, out, land, first_s, first_r)
        if rest is not None:
            for k in range(first + by, last + by, by):
                hand(k, rest, rest_land, rest_s, rest_r)

        def wait(dst=land, r_at=first_r):
            @pl.when(layer != first)
            def _():
                for step in range(1, NP):
                    peer = lax.rem(layer + step, NP)
                    arrived(dst.at[peer], r_at + peer)

        def wait_rest():
            wait(rest_land, rest_r)

        def done():
            for src, dst, s_at, r_at in ((out, land, first_s, first_r), (rest, rest_land, rest_s, rest_r)):
                if src is None:
                    continue
                for k in range(first + by, last + by, by):

                    @pl.when(layer != k)
                    def _():
                        pltpu.make_async_remote_copy(
                            src_ref=src.at[k], dst_ref=dst.at[layer], send_sem=send.at[s_at + k],
                            recv_sem=recv.at[r_at + layer], device_id={"layer": k}, device_id_type=MESH,
                        ).wait_send()

        return wait, wait_rest, done

    wait_d, wait_rest, done_d = sweep(0, NP - 1, 1, gf, gc, ga, db, rd, dl, rl)

    @pl.when(layer == 0)
    def _():
        for r in range(TR):
            rd[r], rl[r] = split3(x0[r])

    wait_d()
    for r in range(TR):
        main_n[:, r * TC : (r + 1) * TC] = rd[r]
    pack_edges(main_n, pack_n)
    wait_n = send_halo(main_n, pack_n, TR, rm_n, rp_n)
    wait_at = to_all(layer, "layer", lambda peer: atmap, gat)
    wait_cq = to_all(layer, "layer", lambda peer: q0.at[peer], gq)
    gq[layer] = q0[layer]
    wait_rest()
    for r in range(TR):
        value = jnp.where(layer == 0, x0[r], rd[r].astype(F32) + rl[r].astype(F32))
        n0[r] = value
        ns_ref[0, :, r, :] = value
    wait_q()
    assemble(qw, q0, rm_q, rp_q, 4)

    wait_n()
    assemble(xw, n0, rm_n, rp_n, HALO)
    for number in range(LG):
        forward(number, sa.at[number], ts.at[number], 2 * LG - 1 - number)

    grad_low, grad_high = span(1)
    first_s_rr, first_r_rr = slots(0, NP), slots(1, NP)

    def source_of(number):
        def take(start, size):
            return (
                window_of(qw, start, size)
                * window_of(ts.at[number], start, size)
                * window_of(inside, start, size)[0:1]
            )

        return take

    for number in reversed(range(LG)):
        halo = number
        take = source_of(number)
        spread(take, ss, span(halo + 1))
        for start, size in chunks(span(0)):
            so[:, PAD + start : PAD + start + size] = take(start, size) * window_of(own, start, size)[0:1]
        for start, size in chunks((grad_low, grad_high)):
            to = start - grad_low
            sw[0:CH, to : to + size] = shifted(so, slice(0, CH), start + ST, size).astype(BF16)
            sw[CH : 2 * CH, to : to + size] = window_of(so, start, size).astype(BF16)
            sw[2 * CH : 3 * CH, to : to + size] = shifted(so, slice(0, CH), start - ST, size).astype(BF16)
        grad = lax.dot_general(
            sw[...], sa[number, :, grad_low:grad_high], (((1,), (1,)), ((), ())), preferred_element_type=F32
        )
        packed = jnp.concatenate(
            [grad[:, :128], jnp.concatenate([grad[:96, 128:192], grad[96:, 128:192]], axis=1)], axis=0
        )
        for half in range(2):
            piece = 2 * number + half
            gpf[piece] = packed[half * PIECE : (half + 1) * PIECE]
            gpb[piece] = packed[half * PIECE : (half + 1) * PIECE].astype(BF16)

            @pl.when(row != piece)
            def _():
                push(gpb.at[piece], rr.at[row], first_s_rr + piece, first_r_rr + row, {"row": piece})

        multiply(wback_ref[number], ss, span(halo + 1))
        for start, size in chunks(span(halo)):
            qw[:, PAD + start : PAD + start + size] += gathered(start, size)

    for r in range(TR):
        gb[r] = (tile_row(qw, r) - q0[r]).astype(BF16)
    wait_g = to_all(layer, "layer", lambda peer: gb.at[peer], gg)
    gg[layer] = gb[layer]
    wait_at()
    wait_cq()
    wait_g()
    wait_e, _, done_e = sweep(NP - 1, 0, -1, gg, gq, gat, eb, re)

    total = gpf[row]
    for by in range(1, NP):
        peer = lax.rem(row + by, NP)
        arrived(rr.at[peer], first_r_rr + peer)
        total += rr[peer].astype(F32)
    hb[...] = total.astype(BF16)
    wait_rc = to_all(col, "col", lambda peer: hb, rc)
    rc[col] = hb[...]

    @pl.when(layer == NP - 1)
    def _():
        for r in range(TR):
            na_ref[0, :, r, :] = q0[r]

    @pl.when(layer != NP - 1)
    def _():
        wait_e()
        for r in range(TR):
            na_ref[0, :, r, :] = re[r].astype(F32)

    wait_rc()
    total = rc[0].astype(F32)
    for k in range(1, NP):
        total += rc[k].astype(F32)
    pb[...] = total.astype(BF16)
    wait_all = to_all(row, "row", lambda peer: pb, gall)
    gall[row] = pb[...]
    wait_all()
    for number in range(LG):
        packed = jnp.concatenate([gall[2 * number], gall[2 * number + 1]], axis=0).astype(F32)
        rest = jnp.concatenate([packed[192:, :64], packed[192:, 64:]], axis=0)
        for r in range(3):
            wg_ref[number, :, r * 192 : (r + 1) * 192] = jnp.concatenate(
                [packed[r * CH : (r + 1) * CH], rest[r * CH : (r + 1) * CH]], axis=1
            )

    for copy in finish:
        copy.wait_send()
    done_d()
    done_e()
    for piece in range(NP):

        @pl.when(row != piece)
        def _():
            pltpu.make_async_remote_copy(
                src_ref=gpb.at[piece], dst_ref=rr.at[row], send_sem=send.at[first_s_rr + piece],
                recv_sem=recv.at[first_r_rr + row], device_id={"row": piece}, device_id_type=MESH,
            ).wait_send()


def local(c_states, c_adjoints, weights):
    vm = pltpu.VMEM
    tile = (TR, CH, TC)
    flat = (CH, TR * TC)
    scratch = [
        vm(tile, F32), vm(tile, F32), vm(tile, F32),
        vm(flat, BF16), vm((CH, 128), BF16), vm(flat, BF16), vm((CH, 128), BF16), vm(flat, BF16), vm((CH, 128), BF16),
        vm((2,) + flat, BF16), vm((6, CH, 128), BF16), vm((2,) + flat, BF16), vm((6, CH, 128), BF16),
        vm((2,) + flat, BF16), vm((6, CH, 128), BF16),
        vm((CH, 128), BF16), vm((CH, 128), BF16), vm((NP, CH, 128), BF16), vm((NP, CH, 128), BF16),
        vm(tile, F32), vm(tile, F32), vm(tile, BF16), vm(tile, BF16), vm(tile, BF16), vm(tile, BF16), vm(tile, BF16), vm(tile, BF16),
        vm(tile, BF16), vm(tile, BF16), vm(tile, BF16), vm(tile, BF16),
        vm((8, WIDE), F32), vm((8, WIDE), F32), vm((CH, WIDE), F32), vm((CH, WIDE), F32),
        vm((3 * CH, WIDE), F32), vm((LG, 3 * CH, LEN), BF16), vm((LG, CH, WIDE), F32),
        vm((3 * CH, LEN), BF16), vm((CH, WIDE), F32), vm((3 * CH, span(1)[1] - span(1)[0]), BF16),
        vm((NP, PIECE, 128), F32), vm((NP, PIECE, 128), BF16), vm((NP, PIECE, 128), BF16),
        vm((PIECE, 128), BF16), vm((NP, PIECE, 128), BF16), vm((PIECE, 128), BF16), vm((NP, PIECE, 128), BF16),
        pltpu.SemaphoreType.DMA((128,)), pltpu.SemaphoreType.DMA((128,)),
    ]
    taps = weights.reshape(LG, CH, 3, 3, CH)
    ahead = jnp.transpose(weights.reshape(LG, CH, 3, 3 * CH), (0, 2, 1, 3)).reshape(LG, 3 * CH, 3 * CH)
    back = jnp.transpose(taps[:, :, ::-1, ::-1, :], (0, 2, 4, 3, 1)).reshape(LG, 3 * CH, 3 * CH)
    return pl.pallas_call(
        body,
        out_shape=(
            jax.ShapeDtypeStruct(c_states.shape, F32),
            jax.ShapeDtypeStruct(c_states.shape, F32),
            jax.ShapeDtypeStruct(weights.shape, F32),
        ),
        in_specs=[pl.BlockSpec(memory_space=pltpu.VMEM)] * 5,
        out_specs=[pl.BlockSpec(memory_space=pltpu.VMEM)] * 3,
        scratch_shapes=scratch,
        compiler_params=pltpu.CompilerParams(
            collective_id=0, has_side_effects=True, vmem_limit_bytes=48 * 1024 * 1024
        ),
    )(c_states, c_adjoints, weights, ahead, back)


def solution(mesh):
    placed = (P("layer", None, "row", "col"), P("layer", None, "row", "col"), P("layer", None, None))
    return jax.shard_map(local, mesh=mesh, in_specs=placed, out_specs=placed, check_vma=False)
```

time: 563 us -> 84.8 us (0.15)
  waiting for transfers between devices: 312 us -> 0 us
  starting transfers between devices: 164 us -> 0 us
  Pallas kernels: 0 us -> 77.3 us
  other arithmetic: 24.9 us -> 0 us
  local copies, waits for them, and re-layouts: 28.5 us -> 6.64 us
  between operations: 16.1 us -> 0.7 us
  matrix products: 13.7 us -> 0 us
    ppermute x62 -> x0, waiting for transfers between devices: 202 us -> none  [the longest x14 88.8 us: from_behind(): return lax.ppermute(array, axis, pairs)]
    ppermute x62 -> x0, starting transfers between devices: 164 us -> none  [the longest x24 77.9 us: with_halo(): lax.ppermute(tail, axis, [(i, (i + 1) % count) for i in range(ends)])]
    psum x1 -> x0, waiting for transfers between devices: 110 us -> none  [local(): weight_grads = lax.psum(jnp.stack(grad_list, 0), ('row', 'col'))]
    pallas_call x0 -> x1, Pallas kernels: none -> 77.3 us  [local(): pl.pallas_call(body, out_shape=(jax.ShapeDtypeStruct(c_states.shape, F32)...]
    concatenate x36 -> x0, other arithmetic: 21.9 us -> none  [with_halo(): jnp.concatenate([lax.ppermute(tail, axis, [(i, (i + 1) % count) for i in...]
    dot_general x32 -> x0, matrix products: 13.7 us -> none  [the longest x16 5.85 us: exact_dot(): jnp.dot(left_mat, right_mat, precision=lax.Precision.HIGHEST, preferred_e...]
    unnamed x163 -> x10, local copies, waits for them, and re-layouts: 13.8 us -> 4.01 us
    transpose x8 -> x3, local copies, waits for them, and re-layouts: 7.89 us -> 0.61 us  [the longest x2 0.55 us: local(): jnp.transpose(taps[:, :, ::-1, ::-1, :], (0, 2, 4, 3, 1))]
  transfers between devices with their start and end apart: 63 -> 0, of which waited for: 49 -> 0; matrix products, arithmetic and copies ran while one was open for 5% -> 0% of each run, Pallas kernels for 0% -> 0%
where the time goes in v1:
time: 84.8 us; the launch traced here: 84.6 us
  Pallas kernels  77.3 us (91%)
  local copies, waits for them, and re-layouts  6.64 us (8%)
    pallas_call x1, Pallas kernels, local(): pl.pallas_call(body, out_shape=(jax.ShapeDtypeStruct(c_states.shape, F32)...  77.3 us
    unnamed x10, local copies, waits for them, and re-layouts  4.01 us

profile of v1, /device:TPU:1, one launch (start us, length us, event | category | flops | bytes accessed | tf_op | source)
XLA Modules:
  0.0 84.6 jit_solution(715343557590385606)
XLA Ops:
  0.6 1.6 %reshape.18 = bf16[4,64,3,192]{3,2,1,0:T(4,128)(2,1)S(1)} reshape(bf16[4,64,576]{2,1,0:T(8,128)(2,1)} %w_ref.1) | data formatting | bytes 589824 | tf_op jit(solution)/shard_map/reshape | solution.py:479
  2.2 0.0 copy-start
  2.2 0.1 copy.8
  2.3 0.9 %copy-done = bf16[4,64,576]{2,1,0:T(8,128)(2,1)S(1)} copy-done((bf16[4,64,576]{2,1,0:T(8,128)(2,1)S(1)}, bf16[4,64,576]{2,1,0:T(8,128)(2,1)}, u32[]{:S(2)}) %copy-start) | copy-done | bytes 294936
  3.2 0.3 copy.9
  3.5 0.5 copy.10
  4.1 0.0 copy-start.1
  4.1 0.0 copy-start.2
  4.1 0.4 reshape.21.wback_ref
  4.5 0.5 copy-done.1
  5.0 0.1 copy-done.2
  5.1 77.3 %shard_map.58 = (f32[1,64,8,128]{3,2,1,0:T(8,128)S(1)}, f32[1,64,8,128]{3,2,1,0:T(8,128)S(1)}, f32[4,64,576]{2,1,0:T(8,128)S(1)}) custom-call(f32[1,64,8,128]{3,2,1,0:T(8,128)S(1)} %copy-done.1, f32[1,64,8,128]{3,2,1,0:T(8,128)S(1)} %copy-done.2, bf16[4,64,576]{2,1,0:T(8,128)(2,1)S(1)} %copy-done, bf16[4,192,192]{2,1,0:T(8,128)(2,1)S(1)} %bitcast.5, ...), custom_call_target="tpu_custom_call" | custom-call | tf_op jit(solution)/shard_map/pallas_call | solution.py:481
  82.4 0.7 copy.14
  83.1 0.7 copy.15
  83.8 0.8 copy.16
  (1 shorter events, 0.0 us)
Async XLA Ops:
  2.2 1.0 %copy-start = (bf16[4,64,576]{2,1,0:T(8,128)(2,1)S(1)}, bf16[4,64,576]{2,1,0:T(8,128)(2,1)}, u32[]{:S(2)}) copy-start(bf16[4,64,576]{2,1,0:T(8,128)(2,1)} %w_ref.1) | copy-start | bytes 884740
  4.1 1.0 %copy-start.1 = (f32[1,64,8,128]{3,2,1,0:T(8,128)S(1)}, f32[1,64,8,128]{3,2,1,0:T(8,128)}, u32[]{:S(2)}) copy-start(f32[1,64,8,128]{3,2,1,0:T(8,128)} %x_in.1) | copy-start | bytes 786436
  4.1 1.0 %copy-start.2 = (f32[1,64,8,128]{3,2,1,0:T(8,128)S(1)}, f32[1,64,8,128]{3,2,1,0:T(8,128)}, u32[]{:S(2)}) copy-start(f32[1,64,8,128]{3,2,1,0:T(8,128)} %q_in.1) | copy-start | bytes 786436

commit v2 on v1

--- a/solution.py
+++ b/solution.py
@@ -55,12 +55,12 @@
 
 
 def body(
-    x_in, q_in, w_ref, wall_ref, wback_ref,
+    x_in, q_in, w_ref,
     ns_ref, na_ref, wg_ref,
     x0, q0, n0, main_x, pack_x, main_q, pack_q, main_n, pack_n,
     rm_x, rp_x, rm_q, rp_q, rm_n, rp_n,
     amap, atmap, ga, gat, gc, gq, fb, gf, db, rd, dl, rl, gb, gg, eb, re,
-    inside, own, xw, qw, yw, sa, ts, ss, so, sw,
+    wall, wback, inside, own, xw, qw, yw, sa, ts, ss, so, sw,
     gpf, gpb, rr, hb, rc, pb, gall,
     send, recv,
 ):
@@ -175,13 +175,6 @@
     gat[layer] = atmap[...]
     gc[layer] = x0[layer]
 
-    for r in range(TR):
-        value = q_in[0, :, r, :]
-        q0[r] = value
-        main_q[:, r * TC : (r + 1) * TC] = value.astype(BF16)
-    pack_edges(main_q, pack_q)
-    wait_q = send_halo(main_q, pack_q, 4, rm_q, rp_q)
-
     place = lax.broadcasted_iota(jnp.int32, (8, WIDE), 1)
     lanes = place - PAD
     held = (lanes >= 0) & (lanes < LEN)
@@ -192,10 +185,11 @@
     inside[...] = ok.astype(F32)
     mine = held & (r_at >= 0) & (r_at < TR) & (c_at >= 0) & (c_at < TC)
     own[...] = mine.astype(F32)
-    for ref in (xw, qw):
-        ref[...] = jnp.zeros_like(ref)
+    xw[...] = jnp.zeros_like(xw)
     yw[...] = jnp.zeros_like(yw)
-    so[...] = jnp.zeros_like(so)
+    for number in range(LG):
+        for r in range(3):
+            wall[number, r * CH : (r + 1) * CH, :] = w_ref[number, :, r * 192 : (r + 1) * 192]
 
     def assemble(ref, tile, rm, rp, halo):
         sides = ((rp[2], rp[3]), (rp[0], rp[1]), (rp[4], rp[5]))
@@ -217,14 +211,12 @@
             )
 
     def spread(take, dst, bounds):
-        for start, size in chunks(bounds):
-            window = take(start - 128, size + 256)
+        for start, size in chunks(bounds, 512):
             width = size + 256
-            dst[0:CH, start : start + size] = pltpu.roll(window, 1, 1)[:, 128 : 128 + size].astype(BF16)
-            dst[CH : 2 * CH, start : start + size] = window[:, 128 : 128 + size].astype(BF16)
-            dst[2 * CH : 3 * CH, start : start + size] = pltpu.roll(window, width - 1, 1)[
-                :, 128 : 128 + size
-            ].astype(BF16)
+            window = take(start - 128, width).astype(BF16)
+            dst[0:CH, start : start + size] = pltpu.roll(window[:, : size + 128], 1, 1)[:, 128 : 128 + size]
+            dst[CH : 2 * CH, start : start + size] = window[:, 128 : 128 + size]
+            dst[2 * CH : 3 * CH, start : start + size] = pltpu.roll(window[:, 128:], size + 127, 1)[:, :size]
 
     def multiply(matrix, src, bounds):
         for start, size in chunks(bounds):
@@ -245,8 +237,8 @@
 
     def forward(number, cols, slopes, halo):
         spread(masked_state, cols, span(halo + 1))
-        multiply(wall_ref[number], cols, span(halo + 1))
-        for start, size in chunks(span(halo)):
+        multiply(wall[number], cols, span(halo + 1))
+        for start, size in chunks(span(halo), 1024):
             bent = jnp.tanh(gathered(start, size))
             xw[:, PAD + start : PAD + start + size] += step_size * bent
             if slopes is not None:
@@ -263,6 +255,26 @@
         fb[r] = (tile_row(xw, r) - x0[r]).astype(BF16)
     wait_f = to_all(layer, "layer", lambda peer: fb.at[peer], gf)
     gf[layer] = fb[layer]
+    for r in range(TR):
+        value = q_in[0, :, r, :]
+        q0[r] = value
+        main_q[:, r * TC : (r + 1) * TC] = value.astype(BF16)
+    pack_edges(main_q, pack_q)
+    wait_q = send_halo(main_q, pack_q, 4, rm_q, rp_q)
+
+    qw[...] = jnp.zeros_like(qw)
+    so[...] = jnp.zeros_like(so)
+    same = (
+        lax.broadcasted_iota(jnp.int32, (3 * CH, 3 * CH), 0) == lax.broadcasted_iota(jnp.int32, (3 * CH, 3 * CH), 1)
+    ).astype(F32).astype(BF16)
+    for number in range(LG):
+        for r in range(3):
+            turned = lax.dot_general(
+                same, wall[number, r * CH : (r + 1) * CH, :], (((1,), (1,)), ((), ())), preferred_element_type=F32
+            )
+            wback[number, (2 - r) * CH : (3 - r) * CH, :] = jnp.concatenate(
+                [turned[2 * CH :], turned[CH : 2 * CH], turned[:CH]], axis=1
+            ).astype(BF16)
     wait_a()
     wait_c()
     wait_f()
@@ -393,19 +405,14 @@
             def _():
                 push(gpb.at[piece], rr.at[row], first_s_rr + piece, first_r_rr + row, {"row": piece})
 
-        multiply(wback_ref[number], ss, span(halo + 1))
-        for start, size in chunks(span(halo)):
+        multiply(wback[number], ss, span(halo + 1))
+        for start, size in chunks(span(halo), 1024):
             qw[:, PAD + start : PAD + start + size] += gathered(start, size)
 
     for r in range(TR):
         gb[r] = (tile_row(qw, r) - q0[r]).astype(BF16)
     wait_g = to_all(layer, "layer", lambda peer: gb.at[peer], gg)
     gg[layer] = gb[layer]
-    wait_at()
-    wait_cq()
-    wait_g()
-    wait_e, _, done_e = sweep(NP - 1, 0, -1, gg, gq, gat, eb, re)
-
     total = gpf[row]
     for by in range(1, NP):
         peer = lax.rem(row + by, NP)
@@ -415,16 +422,10 @@
     wait_rc = to_all(col, "col", lambda peer: hb, rc)
     rc[col] = hb[...]
 
-    @pl.when(layer == NP - 1)
-    def _():
-        for r in range(TR):
-            na_ref[0, :, r, :] = q0[r]
-
-    @pl.when(layer != NP - 1)
-    def _():
-        wait_e()
-        for r in range(TR):
-            na_ref[0, :, r, :] = re[r].astype(F32)
+    wait_at()
+    wait_cq()
+    wait_g()
+    wait_e, _, done_e = sweep(NP - 1, 0, -1, gg, gq, gat, eb, re)
 
     wait_rc()
     total = rc[0].astype(F32)
@@ -433,6 +434,17 @@
     pb[...] = total.astype(BF16)
     wait_all = to_all(row, "row", lambda peer: pb, gall)
     gall[row] = pb[...]
+    @pl.when(layer == NP - 1)
+    def _():
+        for r in range(TR):
+            na_ref[0, :, r, :] = q0[r]
+
+    @pl.when(layer != NP - 1)
+    def _():
+        wait_e()
+        for r in range(TR):
+            na_ref[0, :, r, :] = re[r].astype(F32)
+
     wait_all()
     for number in range(LG):
         packed = jnp.concatenate([gall[2 * number], gall[2 * number + 1]], axis=0).astype(F32)
@@ -468,6 +480,7 @@
         vm((CH, 128), BF16), vm((CH, 128), BF16), vm((NP, CH, 128), BF16), vm((NP, CH, 128), BF16),
         vm(tile, F32), vm(tile, F32), vm(tile, BF16), vm(tile, BF16), vm(tile, BF16), vm(tile, BF16), vm(tile, BF16), vm(tile, BF16),
         vm(tile, BF16), vm(tile, BF16), vm(tile, BF16), vm(tile, BF16),
+        vm((LG, 3 * CH, 3 * CH), BF16), vm((LG, 3 * CH, 3 * CH), BF16),
         vm((8, WIDE), F32), vm((8, WIDE), F32), vm((CH, WIDE), F32), vm((CH, WIDE), F32),
         vm((3 * CH, WIDE), F32), vm((LG, 3 * CH, LEN), BF16), vm((LG, CH, WIDE), F32),
         vm((3 * CH, LEN), BF16), vm((CH, WIDE), F32), vm((3 * CH, span(1)[1] - span(1)[0]), BF16),
@@ -475,9 +488,6 @@
         vm((PIECE, 128), BF16), vm((NP, PIECE, 128), BF16), vm((PIECE, 128), BF16), vm((NP, PIECE, 128), BF16),
         pltpu.SemaphoreType.DMA((128,)), pltpu.SemaphoreType.DMA((128,)),
     ]
-    taps = weights.reshape(LG, CH, 3, 3, CH)
-    ahead = jnp.transpose(weights.reshape(LG, CH, 3, 3 * CH), (0, 2, 1, 3)).reshape(LG, 3 * CH, 3 * CH)
-    back = jnp.transpose(taps[:, :, ::-1, ::-1, :], (0, 2, 4, 3, 1)).reshape(LG, 3 * CH, 3 * CH)
     return pl.pallas_call(
         body,
         out_shape=(
@@ -485,13 +495,13 @@
             jax.ShapeDtypeStruct(c_states.shape, F32),
             jax.ShapeDtypeStruct(weights.shape, F32),
         ),
-        in_specs=[pl.BlockSpec(memory_space=pltpu.VMEM)] * 5,
+        in_specs=[pl.BlockSpec(memory_space=pltpu.VMEM)] * 3,
         out_specs=[pl.BlockSpec(memory_space=pltpu.VMEM)] * 3,
         scratch_shapes=scratch,
         compiler_params=pltpu.CompilerParams(
             collective_id=0, has_side_effects=True, vmem_limit_bytes=48 * 1024 * 1024
         ),
-    )(c_states, c_adjoints, weights, ahead, back)
+    )(c_states, c_adjoints, weights)
 
 
 def solution(mesh):

time: 84.8 us -> 73.9 us (0.87)
  Pallas kernels: 77.3 us -> 67.4 us
  local copies, waits for them, and re-layouts: 6.64 us -> 5.11 us
    pallas_call x1, Pallas kernels: 77.3 us -> 67.4 us  [local(): pl.pallas_call(body, out_shape=(jax.ShapeDtypeStruct(c_states.shape, F32)...]
    reshape x2 -> x0, local copies, waits for them, and re-layouts: 2.02 us -> none  [the longest x1 1.58 us: local(): weights.reshape(LG, CH, 3, 3 * CH)]
    unnamed x10 -> x9, local copies, waits for them, and re-layouts: 4.01 us -> 5.11 us
where the time goes in v2:
time: 73.9 us; the launch traced here: 73.2 us
  Pallas kernels  67.4 us (91%)
  local copies, waits for them, and re-layouts  5.11 us (7%)
    pallas_call x1, Pallas kernels, local(): pl.pallas_call(body, out_shape=(jax.ShapeDtypeStruct(c_states.shape, F32)...  67.4 us
    unnamed x9, local copies, waits for them, and re-layouts  5.11 us

profile of v2, /device:TPU:1, one launch (start us, length us, event | category | flops | bytes accessed | tf_op | source)
XLA Modules:
  0.0 73.2 jit_solution(12082176277940627476)
XLA Ops:
  0.6 0.0 copy-start
  0.6 1.0 %copy-done = bf16[4,64,576]{2,1,0:T(8,128)(2,1)S(1)} copy-done((bf16[4,64,576]{2,1,0:T(8,128)(2,1)S(1)}, bf16[4,64,576]{2,1,0:T(8,128)(2,1)}, u32[]{:S(2)}) %copy-start) | copy-done | bytes 294936
  1.6 0.0 copy-start.1
  1.6 0.9 %copy-done.1 = f32[1,64,8,128]{3,2,1,0:T(8,128)S(1)} copy-done((f32[1,64,8,128]{3,2,1,0:T(8,128)S(1)}, f32[1,64,8,128]{3,2,1,0:T(8,128)}, u32[]{:S(2)}) %copy-start.1) | copy-done | bytes 262168
  2.6 0.0 copy-start.2
  2.6 0.9 %copy-done.2 = f32[1,64,8,128]{3,2,1,0:T(8,128)S(1)} copy-done((f32[1,64,8,128]{3,2,1,0:T(8,128)S(1)}, f32[1,64,8,128]{3,2,1,0:T(8,128)}, u32[]{:S(2)}) %copy-start.2) | copy-done | bytes 262168
  3.5 67.4 %shard_map.58 = (f32[1,64,8,128]{3,2,1,0:T(8,128)S(1)}, f32[1,64,8,128]{3,2,1,0:T(8,128)S(1)}, f32[4,64,576]{2,1,0:T(8,128)S(1)}) custom-call(f32[1,64,8,128]{3,2,1,0:T(8,128)S(1)} %copy-done.1, f32[1,64,8,128]{3,2,1,0:T(8,128)S(1)} %copy-done.2, bf16[4,64,576]{2,1,0:T(8,128)(2,1)S(1)} %copy-done), custom_call_target="tpu_custom_call" | custom-call | tf_op jit(solution)/shard_map/pallas_call | solution.py:491
  71.0 0.7 copy.9
  71.7 0.7 copy.10
  72.4 0.8 %copy.11 = f32[4,64,576]{2,1,0:T(8,128)} copy(f32[4,64,576]{2,1,0:T(8,128)S(1)} %get-tuple-element.8) | data formatting | bytes 1179648
Async XLA Ops:
  0.6 1.0 %copy-start = (bf16[4,64,576]{2,1,0:T(8,128)(2,1)S(1)}, bf16[4,64,576]{2,1,0:T(8,128)(2,1)}, u32[]{:S(2)}) copy-start(bf16[4,64,576]{2,1,0:T(8,128)(2,1)} %w_ref.1) | copy-start | bytes 884740
  1.6 0.9 %copy-start.1 = (f32[1,64,8,128]{3,2,1,0:T(8,128)S(1)}, f32[1,64,8,128]{3,2,1,0:T(8,128)}, u32[]{:S(2)}) copy-start(f32[1,64,8,128]{3,2,1,0:T(8,128)} %x_in.1) | copy-start | bytes 786436
  2.6 0.9 %copy-start.2 = (f32[1,64,8,128]{3,2,1,0:T(8,128)S(1)}, f32[1,64,8,128]{3,2,1,0:T(8,128)}, u32[]{:S(2)}) copy-start(f32[1,64,8,128]{3,2,1,0:T(8,128)} %q_in.1) | copy-start | bytes 786436

commit v3 on v2

--- a/solution.py
+++ b/solution.py
@@ -17,35 +17,18 @@
 TC = 128
 NP = 8
 HALO = 8
-ST = TC + 2 * HALO
 RW = TR + 2 * HALO
-LEN = RW * ST
-PAD = 256
-WIDE = LEN + 2 * PAD
+MAIN = RW * TC
+SIDE = RW * 2 * HALO
+LEN = MAIN + SIDE
+BLOCKS = RW // TR
 NEAR = ((0, -1), (0, 1), (-1, -1), (-1, 1), (1, -1), (1, 1))
 PIECE = 144
 step_size = 0.2
 
 
-def span(halo):
-    low, high = (HALO - halo) * ST, (HALO + TR + halo) * ST
-    return low // 128 * 128, -(-high // 128) * 128
-
-
-def chunks(bounds, size=256):
-    low, high = bounds
+def chunks(low, high, size):
     return [(at, min(size, high - at)) for at in range(low, high, size)]
-
-
-def shifted(ref, rows, start, size):
-    begin = start + PAD
-    low = begin // 128 * 128
-    off = begin - low
-    if off == 0:
-        return ref[rows, low : low + size]
-    width = size + 128
-    window = ref[rows, low : low + width]
-    return pltpu.roll(window, width - off, 1)[:, :size]
 
 
 def split3(matrix):
@@ -55,14 +38,14 @@
 
 
 def body(
-    x_in, q_in, w_ref,
-    ns_ref, na_ref, wg_ref,
-    x0, q0, n0, main_x, pack_x, main_q, pack_q, main_n, pack_n,
+    x_hbm, q_hbm, w_hbm,
+    ns_hbm, na_hbm, wg_hbm,
+    ns_ref, na_ref, wg_ref, x_in, q_in, w_ref, x0, q0, n0, main_x, pack_x, main_q, pack_q, main_n, pack_n,
     rm_x, rp_x, rm_q, rp_q, rm_n, rp_n,
     amap, atmap, ga, gat, gc, gq, fb, gf, db, rd, dl, rl, gb, gg, eb, re,
-    wall, wback, inside, own, xw, qw, yw, sa, ts, ss, so, sw,
-    gpf, gpb, rr, hb, rc, pb, gall,
-    send, recv,
+    wall, wback, xw, qw, yw, sa, ts, ss, sw,
+    gpf, gpb, rr, hb, share, common, mine, joined, pb, gall,
+    send, recv, fetch,
 ):
     layer, row, col = (lax.axis_index(name) for name in ("layer", "row", "col"))
     finish = []
@@ -89,6 +72,13 @@
             src_ref=dst, dst_ref=dst, send_sem=send.at[0], recv_sem=recv.at[recv_at],
             device_id={"layer": layer}, device_id_type=MESH,
         ).wait_recv()
+
+    fetches = [
+        pltpu.make_async_copy(src, dst, fetch.at[number])
+        for number, (src, dst) in enumerate(((x_hbm, x_in), (w_hbm, w_ref), (q_hbm, q_in)))
+    ]
+    for copy in fetches:
+        copy.start()
 
     barrier = pltpu.get_barrier_semaphore()
     for by in range(1, NP):
@@ -102,13 +92,14 @@
     spot = lax.broadcasted_iota(jnp.int32, (TR * TC, 128), 0)
     lane = lax.broadcasted_iota(jnp.int32, (TR * TC, 128), 1)
     column, line = spot % TC, spot // TC
-    picks = (lane < 64) & (column < HALO) & (lane == line * HALO + column)
-    picks |= (lane >= 64) & (column >= TC - HALO) & (lane - 64 == line * HALO + column - (TC - HALO))
+    wanted = jnp.where(lane % 16 < HALO, TC - HALO + lane % 16, lane % 16 - HALO)
+    picks = (lane // 16 == line) & (column == wanted)
     edges = picks.astype(F32).astype(BF16)
 
     def pack_edges(main, pack):
         pack[...] = jnp.dot(main[...], edges, preferred_element_type=F32).astype(BF16)
 
+    fetches[0].wait()
     for r in range(TR):
         value = x_in[0, :, r, :]
         x0[r] = value
@@ -165,6 +156,7 @@
     eye = (
         lax.broadcasted_iota(jnp.int32, (CH, CH), 0) == lax.broadcasted_iota(jnp.int32, (CH, CH), 1)
     ).astype(F32)
+    fetches[1].wait()
     summed = jnp.dot(w_ref[0], fold, preferred_element_type=F32)
     summed_t = lax.dot_general(fold_t, w_ref[0], (((1,), (1,)), ((), ())), preferred_element_type=F32)
     amap[...] = jnp.concatenate(split3(eye + step_size * summed), axis=1)
@@ -175,77 +167,104 @@
     gat[layer] = atmap[...]
     gc[layer] = x0[layer]
 
-    place = lax.broadcasted_iota(jnp.int32, (8, WIDE), 1)
-    lanes = place - PAD
-    held = (lanes >= 0) & (lanes < LEN)
-    safe = jnp.where(held, lanes, 0)
-    r_at, c_at = safe // ST - HALO, safe % ST - HALO
-    r_all, c_all = row * TR + r_at, col * TC + c_at
-    ok = held & (r_all >= 0) & (r_all < NP * TR) & (c_all >= 0) & (c_all < NP * TC)
-    inside[...] = ok.astype(F32)
-    mine = held & (r_at >= 0) & (r_at < TR) & (c_at >= 0) & (c_at < TC)
-    own[...] = mine.astype(F32)
-    xw[...] = jnp.zeros_like(xw)
-    yw[...] = jnp.zeros_like(yw)
+    block_ok = ((row > 0).astype(F32), None, (row < NP - 1).astype(F32))
+    lane_in_row = lax.broadcasted_iota(jnp.int32, (1, 128), 1) % 16
+    side_ok = jnp.where(lane_in_row < HALO, (col > 0).astype(F32), (col < NP - 1).astype(F32))
+    lane_at = lax.broadcasted_iota(jnp.int32, (CH, 128), 1)
+    lane_bf = lane_at.astype(F32).astype(BF16)
+    lane16_bf = (lane_at % 16).astype(F32).astype(BF16)
+    last_lane, first_lane = lane_bf == 127, lane_bf == 0
+    left_end, right_end = lane16_bf == HALO - 1, lane16_bf == HALO
+    o_row = lax.broadcasted_iota(jnp.int32, (128, TR * TC), 0)
+    o_lane = lax.broadcasted_iota(jnp.int32, (128, TR * TC), 1)
+    outward = (((o_lane % TC == 0) & (o_row == o_lane // TC * 16 + 7)) | ((o_lane % TC == 127) & (o_row == o_lane // TC * 16 + 8))).astype(F32).astype(BF16)
+    pick0 = (lane_at == 0).astype(F32).astype(BF16)
+    pick1 = (lane_at == 127).astype(F32).astype(BF16)
+    keep0 = (lane_at != 0).astype(F32).astype(BF16)
+    keep1 = (lane_at != 127).astype(F32).astype(BF16)
+    on_left = lane_at % 16 < HALO
     for number in range(LG):
         for r in range(3):
             wall[number, r * CH : (r + 1) * CH, :] = w_ref[number, :, r * 192 : (r + 1) * 192]
 
     def assemble(ref, tile, rm, rp, halo):
-        sides = ((rp[2], rp[3]), (rp[0], rp[1]), (rp[4], rp[5]))
+        sides = ((2, 3), (0, 1), (4, 5))
         for line in range(HALO - halo, HALO + TR + halo):
             block, r = line // TR, line % TR
-            start = PAD + line * ST
-            if block == 1:
-                main = tile[r]
-            else:
-                main = rm[block // 2, :, r * TC : (r + 1) * TC].astype(F32)
-            left, right = sides[block]
-            ref[:, start : start + ST] = jnp.concatenate(
-                [
-                    left[:, 64 + r * HALO : 64 + (r + 1) * HALO].astype(F32),
-                    main,
-                    right[:, r * HALO : (r + 1) * HALO].astype(F32),
-                ],
-                axis=1,
+            main = tile[r] if block == 1 else rm[block // 2, :, r * TC : (r + 1) * TC].astype(F32)
+            ref[:, line * TC : (line + 1) * TC] = main
+        for block, (left, right) in enumerate(sides):
+            start = MAIN + block * 128
+            ref[:, start : start + 128] = jnp.where(on_left, rp[left].astype(F32), rp[right].astype(F32))
+
+    def spread(take, dst, low, high):
+        def put(start, values):
+            for s, value in enumerate(values):
+                dst[s * CH : (s + 1) * CH, start : start + 128] = value
+
+        for block in range(BLOCKS):
+            ok = block_ok[block]
+            side = take(MAIN + block * 128) * side_ok
+            side = (side if ok is None else side * ok).astype(BF16)
+            crossing = jnp.zeros((CH, 128), BF16)
+            arounds = jnp.dot(side, outward, preferred_element_type=F32).astype(BF16)
+            for r in range(TR):
+                line = block * TR + r
+                if not low <= line < high:
+                    continue
+                main = take(line * TC)
+                main = (main if ok is None else main * ok).astype(BF16)
+                put(
+                    line * TC,
+                    (
+                        pltpu.roll(main, 1, 1) * keep0 + arounds[:, r * 128 : (r + 1) * 128] * pick0,
+                        main,
+                        pltpu.roll(main, 127, 1) * keep1 + arounds[:, r * 128 : (r + 1) * 128] * pick1,
+                    ),
+                )
+                beside = pltpu.roll(main, (16 * r + 8) % 128, 1)
+                here = (lane_bf == 16 * r + 7) | (lane_bf == 16 * r + 8)
+                crossing = jnp.where(here, beside, crossing)
+            put(
+                MAIN + block * 128,
+                (
+                    pltpu.roll(jnp.where(left_end, crossing, side), 1, 1),
+                    side,
+                    pltpu.roll(jnp.where(right_end, crossing, side), 127, 1),
+                ),
             )
 
-    def spread(take, dst, bounds):
-        for start, size in chunks(bounds, 512):
-            width = size + 256
-            window = take(start - 128, width).astype(BF16)
-            dst[0:CH, start : start + size] = pltpu.roll(window[:, : size + 128], 1, 1)[:, 128 : 128 + size]
-            dst[CH : 2 * CH, start : start + size] = window[:, 128 : 128 + size]
-            dst[2 * CH : 3 * CH, start : start + size] = pltpu.roll(window[:, 128:], size + 127, 1)[:, :size]
-
-    def multiply(matrix, src, bounds):
-        for start, size in chunks(bounds):
-            yw[:, PAD + start : PAD + start + size] = jnp.dot(
-                matrix, src[:, start : start + size], preferred_element_type=F32
+    def multiply(matrix, src, low, high):
+        for start, size in chunks(low * TC, high * TC, 256) + chunks(MAIN, LEN, 256):
+            yw[:, start : start + size] = jnp.dot(matrix, src[:, start : start + size], preferred_element_type=F32)
+
+    def gathered(low, high):
+        for start, size in chunks(low * TC, high * TC, 256):
+            yield (
+                start,
+                size,
+                yw[:CH, start - TC : start - TC + size]
+                + yw[CH : 2 * CH, start : start + size]
+                + yw[2 * CH :, start + TC : start + TC + size],
             )
-
-    def gathered(start, size):
-        total = yw[CH : 2 * CH, PAD + start : PAD + start + size]
-        total += shifted(yw, slice(0, CH), start - ST, size)
-        return total + shifted(yw, slice(2 * CH, 3 * CH), start + ST, size)
-
-    def window_of(ref, start, size):
-        return ref[:, PAD + start : PAD + start + size]
-
-    def masked_state(start, size):
-        return window_of(xw, start, size) * window_of(inside, start, size)[0:1]
+        yield (
+            MAIN,
+            SIDE,
+            pltpu.roll(yw[:CH, MAIN:], 16, 1) + yw[CH : 2 * CH, MAIN:] + pltpu.roll(yw[2 * CH :, MAIN:], SIDE - 16, 1),
+        )
 
     def forward(number, cols, slopes, halo):
-        spread(masked_state, cols, span(halo + 1))
-        multiply(wall[number], cols, span(halo + 1))
-        for start, size in chunks(span(halo), 1024):
-            bent = jnp.tanh(gathered(start, size))
-            xw[:, PAD + start : PAD + start + size] += step_size * bent
+        low, high = HALO - halo, HALO + TR + halo
+        spread(lambda start: xw[:, start : start + 128], cols, low - 1, high + 1)
+        multiply(wall[number], cols, low - 1, high + 1)
+        for start, size, total in gathered(low, high):
+            bent = jnp.tanh(total)
+            xw[:, start : start + size] += step_size * bent
             if slopes is not None:
-                slopes[:, PAD + start : PAD + start + size] = step_size * (1.0 - bent * bent)
+                slopes[:, start : start + size] = step_size * (1.0 - bent * bent)
 
     def tile_row(ref, r):
-        return shifted(ref, slice(0, CH), (HALO + r) * ST + HALO, TC)
+        return ref[:, (HALO + r) * TC : (HALO + r + 1) * TC]
 
     wait_x()
     assemble(xw, x0, rm_x, rp_x, 4)
@@ -255,6 +274,7 @@
         fb[r] = (tile_row(xw, r) - x0[r]).astype(BF16)
     wait_f = to_all(layer, "layer", lambda peer: fb.at[peer], gf)
     gf[layer] = fb[layer]
+    fetches[2].wait()
     for r in range(TR):
         value = q_in[0, :, r, :]
         q0[r] = value
@@ -262,8 +282,7 @@
     pack_edges(main_q, pack_q)
     wait_q = send_halo(main_q, pack_q, 4, rm_q, rp_q)
 
-    qw[...] = jnp.zeros_like(qw)
-    so[...] = jnp.zeros_like(so)
+    sw[...] = jnp.zeros_like(sw)
     same = (
         lax.broadcasted_iota(jnp.int32, (3 * CH, 3 * CH), 0) == lax.broadcasted_iota(jnp.int32, (3 * CH, 3 * CH), 1)
     ).astype(F32).astype(BF16)
@@ -358,6 +377,8 @@
         value = jnp.where(layer == 0, x0[r], rd[r].astype(F32) + rl[r].astype(F32))
         n0[r] = value
         ns_ref[0, :, r, :] = value
+    stores = [pltpu.make_async_copy(ns_ref, ns_hbm, fetch.at[3])]
+    stores[0].start()
     wait_q()
     assemble(qw, q0, rm_q, rp_q, 4)
 
@@ -366,32 +387,18 @@
     for number in range(LG):
         forward(number, sa.at[number], ts.at[number], 2 * LG - 1 - number)
 
-    grad_low, grad_high = span(1)
     first_s_rr, first_r_rr = slots(0, NP), slots(1, NP)
 
-    def source_of(number):
-        def take(start, size):
-            return (
-                window_of(qw, start, size)
-                * window_of(ts.at[number], start, size)
-                * window_of(inside, start, size)[0:1]
-            )
-
-        return take
-
     for number in reversed(range(LG)):
-        halo = number
-        take = source_of(number)
-        spread(take, ss, span(halo + 1))
-        for start, size in chunks(span(0)):
-            so[:, PAD + start : PAD + start + size] = take(start, size) * window_of(own, start, size)[0:1]
-        for start, size in chunks((grad_low, grad_high)):
-            to = start - grad_low
-            sw[0:CH, to : to + size] = shifted(so, slice(0, CH), start + ST, size).astype(BF16)
-            sw[CH : 2 * CH, to : to + size] = window_of(so, start, size).astype(BF16)
-            sw[2 * CH : 3 * CH, to : to + size] = shifted(so, slice(0, CH), start - ST, size).astype(BF16)
+        low, high = HALO - number, HALO + TR + number
+        slopes = ts.at[number]
+        spread(lambda start: qw[:, start : start + 128] * slopes[:, start : start + 128], ss, low - 1, high + 1)
+        for r in range(3):
+            start = r * TC
+            sw[r * CH : (r + 1) * CH, start : start + TR * TC] = ss[CH : 2 * CH, HALO * TC : (HALO + TR) * TC]
         grad = lax.dot_general(
-            sw[...], sa[number, :, grad_low:grad_high], (((1,), (1,)), ((), ())), preferred_element_type=F32
+            sw[...], sa[number, :, (HALO - 1) * TC : (HALO + TR + 1) * TC], (((1,), (1,)), ((), ())),
+            preferred_element_type=F32,
         )
         packed = jnp.concatenate(
             [grad[:, :128], jnp.concatenate([grad[:96, 128:192], grad[96:, 128:192]], axis=1)], axis=0
@@ -405,9 +412,9 @@
             def _():
                 push(gpb.at[piece], rr.at[row], first_s_rr + piece, first_r_rr + row, {"row": piece})
 
-        multiply(wback[number], ss, span(halo + 1))
-        for start, size in chunks(span(halo), 1024):
-            qw[:, PAD + start : PAD + start + size] += gathered(start, size)
+        multiply(wback[number], ss, low - 1, high + 1)
+        for start, size, total in gathered(low, high):
+            qw[:, start : start + size] += total
 
     for r in range(TR):
         gb[r] = (tile_row(qw, r) - q0[r]).astype(BF16)
@@ -418,20 +425,33 @@
         peer = lax.rem(row + by, NP)
         arrived(rr.at[peer], first_r_rr + peer)
         total += rr[peer].astype(F32)
-    hb[...] = total.astype(BF16)
-    wait_rc = to_all(col, "col", lambda peer: hb, rc)
-    rc[col] = hb[...]
-
+    for k in range(NP + 1):
+        hb[k] = total[16 * k : 16 * (k + 1)].astype(BF16)
+    wait_share = to_all(col, "col", lambda peer: hb.at[peer], share)
+    wait_rest = to_all(col, "col", lambda peer: hb.at[NP], common)
+    share[col] = hb[col]
+    common[col] = hb[NP]
+
+    def added(parts):
+        sum_of = parts[0].astype(F32)
+        for k in range(1, NP):
+            sum_of += parts[k].astype(F32)
+        return sum_of.astype(BF16)
+
+    wait_share()
+    mine[...] = added(share)
+    wait_mine = to_all(col, "col", lambda peer: mine, joined)
+    joined[col] = mine[...]
     wait_at()
     wait_cq()
     wait_g()
     wait_e, _, done_e = sweep(NP - 1, 0, -1, gg, gq, gat, eb, re)
 
-    wait_rc()
-    total = rc[0].astype(F32)
-    for k in range(1, NP):
-        total += rc[k].astype(F32)
-    pb[...] = total.astype(BF16)
+    wait_rest()
+    wait_mine()
+    pb[NP] = added(common)
+    for k in range(NP):
+        pb[k] = joined[k]
     wait_all = to_all(row, "row", lambda peer: pb, gall)
     gall[row] = pb[...]
     @pl.when(layer == NP - 1)
@@ -445,15 +465,24 @@
         for r in range(TR):
             na_ref[0, :, r, :] = re[r].astype(F32)
 
+    stores.append(pltpu.make_async_copy(na_ref, na_hbm, fetch.at[4]))
+    stores[1].start()
+
     wait_all()
     for number in range(LG):
-        packed = jnp.concatenate([gall[2 * number], gall[2 * number + 1]], axis=0).astype(F32)
+        packed = jnp.concatenate(
+            [gall[2 * number + half, k] for half in range(2) for k in range(NP + 1)], axis=0
+        ).astype(F32)
         rest = jnp.concatenate([packed[192:, :64], packed[192:, 64:]], axis=0)
         for r in range(3):
             wg_ref[number, :, r * 192 : (r + 1) * 192] = jnp.concatenate(
                 [packed[r * CH : (r + 1) * CH], rest[r * CH : (r + 1) * CH]], axis=1
             )
-
+        stores.append(pltpu.make_async_copy(wg_ref.at[number], wg_hbm.at[number], fetch.at[5 + number]))
+        stores[-1].start()
+
+    for copy in stores:
+        copy.wait()
     for copy in finish:
         copy.wait_send()
     done_d()
@@ -468,11 +497,21 @@
             ).wait_send()
 
 
+def place_results(*refs):
+    copies = [pltpu.make_async_copy(refs[k], refs[3 + k], refs[6].at[k]) for k in range(3)]
+    for copy in copies:
+        copy.start()
+    for copy in copies:
+        copy.wait()
+
+
 def local(c_states, c_adjoints, weights):
     vm = pltpu.VMEM
     tile = (TR, CH, TC)
     flat = (CH, TR * TC)
     scratch = [
+        vm(c_states.shape, F32), vm(c_states.shape, F32), vm(weights.shape, F32),
+        vm(c_states.shape, F32), vm(c_states.shape, F32), vm(weights.shape, BF16),
         vm(tile, F32), vm(tile, F32), vm(tile, F32),
         vm(flat, BF16), vm((CH, 128), BF16), vm(flat, BF16), vm((CH, 128), BF16), vm(flat, BF16), vm((CH, 128), BF16),
         vm((2,) + flat, BF16), vm((6, CH, 128), BF16), vm((2,) + flat, BF16), vm((6, CH, 128), BF16),
@@ -481,27 +520,36 @@
         vm(tile, F32), vm(tile, F32), vm(tile, BF16), vm(tile, BF16), vm(tile, BF16), vm(tile, BF16), vm(tile, BF16), vm(tile, BF16),
         vm(tile, BF16), vm(tile, BF16), vm(tile, BF16), vm(tile, BF16),
         vm((LG, 3 * CH, 3 * CH), BF16), vm((LG, 3 * CH, 3 * CH), BF16),
-        vm((8, WIDE), F32), vm((8, WIDE), F32), vm((CH, WIDE), F32), vm((CH, WIDE), F32),
-        vm((3 * CH, WIDE), F32), vm((LG, 3 * CH, LEN), BF16), vm((LG, CH, WIDE), F32),
-        vm((3 * CH, LEN), BF16), vm((CH, WIDE), F32), vm((3 * CH, span(1)[1] - span(1)[0]), BF16),
+        vm((CH, LEN), F32), vm((CH, LEN), F32),
+        vm((3 * CH, LEN), F32), vm((LG, 3 * CH, LEN), BF16), vm((LG, CH, LEN), F32),
+        vm((3 * CH, LEN), BF16), vm((3 * CH, (TR + 2) * TC), BF16),
         vm((NP, PIECE, 128), F32), vm((NP, PIECE, 128), BF16), vm((NP, PIECE, 128), BF16),
-        vm((PIECE, 128), BF16), vm((NP, PIECE, 128), BF16), vm((PIECE, 128), BF16), vm((NP, PIECE, 128), BF16),
-        pltpu.SemaphoreType.DMA((128,)), pltpu.SemaphoreType.DMA((128,)),
+        vm((NP + 1, 16, 128), BF16), vm((NP, 16, 128), BF16), vm((NP, 16, 128), BF16), vm((16, 128), BF16),
+        vm((NP, 16, 128), BF16), vm((NP + 1, 16, 128), BF16), vm((NP, NP + 1, 16, 128), BF16),
+        pltpu.SemaphoreType.DMA((160,)), pltpu.SemaphoreType.DMA((160,)), pltpu.SemaphoreType.DMA((5 + LG,)),
     ]
-    return pl.pallas_call(
+    results = pl.pallas_call(
         body,
         out_shape=(
             jax.ShapeDtypeStruct(c_states.shape, F32),
             jax.ShapeDtypeStruct(c_states.shape, F32),
             jax.ShapeDtypeStruct(weights.shape, F32),
         ),
-        in_specs=[pl.BlockSpec(memory_space=pltpu.VMEM)] * 3,
-        out_specs=[pl.BlockSpec(memory_space=pltpu.VMEM)] * 3,
+        in_specs=[pl.BlockSpec(memory_space=pltpu.HBM)] * 3,
+        out_specs=[pl.BlockSpec(memory_space=pltpu.HBM)] * 3,
         scratch_shapes=scratch,
         compiler_params=pltpu.CompilerParams(
-            collective_id=0, has_side_effects=True, vmem_limit_bytes=48 * 1024 * 1024
+            collective_id=0, has_side_effects=True, vmem_limit_bytes=60 * 1024 * 1024
         ),
     )(c_states, c_adjoints, weights)
+    return pl.pallas_call(
+        place_results,
+        out_shape=tuple(jax.ShapeDtypeStruct(value.shape, F32) for value in results),
+        in_specs=[pl.BlockSpec(memory_space=pltpu.HBM)] * 3,
+        out_specs=[pl.BlockSpec(memory_space=pltpu.HBM)] * 3,
+        scratch_shapes=[pltpu.SemaphoreType.DMA((3,))],
+        compiler_params=pltpu.CompilerParams(vmem_limit_bytes=60 * 1024 * 1024),
+    )(*results)
 
 
 def solution(mesh):

time: 73.9 us -> 106 us (1.43)
  Pallas kernels: 67.4 us -> 105 us
  local copies, waits for them, and re-layouts: 5.11 us -> 0 us
    pallas_call x0 -> x1, Pallas kernels: none -> 36.9 us  [local(): pl.pallas_call(place_results, out_shape=tuple((jax.ShapeDtypeStruct(value...]
    unnamed x9 -> x0, local copies, waits for them, and re-layouts: 5.11 us -> none
where the time goes in v3:
time: 106 us
  Pallas kernels  105 us (99%)
    pallas_call x1, Pallas kernels, local(): pl.pallas_call(body, out_shape=(jax.ShapeDtypeStruct(c_states.shape, F32)...  67.9 us
    pallas_call x1, Pallas kernels, local(): pl.pallas_call(place_results, out_shape=tuple((jax.ShapeDtypeStruct(value...  36.9 us

profile of v3, /device:TPU:1, one launch (start us, length us, event | category | flops | bytes accessed | tf_op | source)
XLA Modules:
  0.0 105.6 jit_solution(11246165583206189494)
XLA Ops:
  0.6 67.9 %shard_map.58 = (f32[1,64,8,128]{3,2,1,0:T(8,128)}, f32[1,64,8,128]{3,2,1,0:T(8,128)}, f32[4,64,576]{2,1,0:T(8,128)}) custom-call(f32[1,64,8,128]{3,2,1,0:T(8,128)} %x_hbm.1, f32[1,64,8,128]{3,2,1,0:T(8,128)} %q_hbm.1, bf16[4,64,576]{2,1,0:T(8,128)(2,1)} %w_hbm.1), custom_call_target="tpu_custom_call" | custom-call | tf_op jit(solution)/shard_map/pallas_call | solution.py:531
  68.6 36.9 %shard_map.59 = (f32[1,64,8,128]{3,2,1,0:T(8,128)}, f32[1,64,8,128]{3,2,1,0:T(8,128)}, f32[4,64,576]{2,1,0:T(8,128)}) custom-call(f32[1,64,8,128]{3,2,1,0:T(8,128)} %get-tuple-element.6.refs_0_, f32[1,64,8,128]{3,2,1,0:T(8,128)} %get-tuple-element.7.refs_1_, f32[4,64,576]{2,1,0:T(8,128)} %get-tuple-element.8.refs_2_), custom_call_target="tpu_custom_call" | custom-call | tf_op jit(solution)/shard_map/pallas_call | solution.py:545

commit v4 on v3

--- a/solution.py
+++ b/solution.py
@@ -498,10 +498,15 @@
 
 
 def place_results(*refs):
-    copies = [pltpu.make_async_copy(refs[k], refs[3 + k], refs[6].at[k]) for k in range(3)]
-    for copy in copies:
+    sources, results, held, arrive, leave = refs[:3], refs[3:6], refs[6:9], refs[9], refs[10]
+    reads = [pltpu.make_async_copy(sources[k], held[k], arrive.at[k]) for k in range(3)]
+    writes = [pltpu.make_async_copy(held[k], results[k], leave.at[k]) for k in range(3)]
+    for copy in reads:
         copy.start()
-    for copy in copies:
+    for read, write in zip(reads, writes):
+        read.wait()
+        write.start()
+    for copy in writes:
         copy.wait()
 
 
@@ -547,7 +552,7 @@
         out_shape=tuple(jax.ShapeDtypeStruct(value.shape, F32) for value in results),
         in_specs=[pl.BlockSpec(memory_space=pltpu.HBM)] * 3,
         out_specs=[pl.BlockSpec(memory_space=pltpu.HBM)] * 3,
-        scratch_shapes=[pltpu.SemaphoreType.DMA((3,))],
+        scratch_shapes=[pltpu.VMEM(value.shape, F32) for value in results] + [pltpu.SemaphoreType.DMA((3,))] * 2,
         compiler_params=pltpu.CompilerParams(vmem_limit_bytes=60 * 1024 * 1024),
     )(*results)
 

time: 106 us -> 71 us (0.67)
  Pallas kernels: 105 us -> 70.1 us
    pallas_call x1, Pallas kernels: 36.9 us -> 2.14 us  [local(): pl.pallas_call(place_results, out_shape=tuple((jax.ShapeDtypeStruct(value...]
where the time goes in v4:
time: 71 us; the launch traced here: 70.9 us
  Pallas kernels  70.1 us (99%)
  between operations  0.8 us (1%)
    pallas_call x1, Pallas kernels, local(): pl.pallas_call(body, out_shape=(jax.ShapeDtypeStruct(c_states.shape, F32)...  67.9 us
    pallas_call x1, Pallas kernels, local(): pl.pallas_call(place_results, out_shape=tuple((jax.ShapeDtypeStruct(value...  2.14 us

profile of v4, /device:TPU:1, one launch (start us, length us, event | category | flops | bytes accessed | tf_op | source)
XLA Modules:
  0.0 70.9 jit_solution(4391615556555314090)
XLA Ops:
  0.6 67.9 %shard_map.58 = (f32[1,64,8,128]{3,2,1,0:T(8,128)}, f32[1,64,8,128]{3,2,1,0:T(8,128)}, f32[4,64,576]{2,1,0:T(8,128)}) custom-call(f32[1,64,8,128]{3,2,1,0:T(8,128)} %x_hbm.1, f32[1,64,8,128]{3,2,1,0:T(8,128)} %q_hbm.1, bf16[4,64,576]{2,1,0:T(8,128)(2,1)} %w_hbm.1), custom_call_target="tpu_custom_call" | custom-call | tf_op jit(solution)/shard_map/pallas_call | solution.py:536
  68.6 2.1 %shard_map.59 = (f32[1,64,8,128]{3,2,1,0:T(8,128)}, f32[1,64,8,128]{3,2,1,0:T(8,128)}, f32[4,64,576]{2,1,0:T(8,128)}) custom-call(f32[1,64,8,128]{3,2,1,0:T(8,128)} %get-tuple-element.6.refs_0_, f32[1,64,8,128]{3,2,1,0:T(8,128)} %get-tuple-element.7.refs_1_, f32[4,64,576]{2,1,0:T(8,128)} %get-tuple-element.8.refs_2_), custom_call_target="tpu_custom_call" | custom-call | tf_op jit(solution)/shard_map/pallas_call | solution.py:550

commit v5 on v4

--- a/solution.py
+++ b/solution.py
@@ -142,6 +142,12 @@
                 peer = lax.rem(which + by, NP)
                 arrived(dst.at[peer], first_r + peer)
 
+        def wait_one(peer):
+            @pl.when(which != peer)
+            def _():
+                arrived(dst.at[peer], first_r + peer)
+
+        wait.one = wait_one
         return wait
 
     pl.semaphore_wait(barrier, 3 * (NP - 1) + 4)
@@ -438,15 +444,15 @@
             sum_of += parts[k].astype(F32)
         return sum_of.astype(BF16)
 
+    wait_at()
+    wait_cq()
+    wait_g()
+    wait_e, _, done_e = sweep(NP - 1, 0, -1, gg, gq, gat, eb, re)
+
     wait_share()
     mine[...] = added(share)
     wait_mine = to_all(col, "col", lambda peer: mine, joined)
     joined[col] = mine[...]
-    wait_at()
-    wait_cq()
-    wait_g()
-    wait_e, _, done_e = sweep(NP - 1, 0, -1, gg, gq, gat, eb, re)
-
     wait_rest()
     wait_mine()
     pb[NP] = added(common)
@@ -468,8 +474,9 @@
     stores.append(pltpu.make_async_copy(na_ref, na_hbm, fetch.at[4]))
     stores[1].start()
 
-    wait_all()
-    for number in range(LG):
+    for number in reversed(range(LG)):
+        for half in range(2):
+            wait_all.one(2 * number + half)
         packed = jnp.concatenate(
             [gall[2 * number + half, k] for half in range(2) for k in range(NP + 1)], axis=0
         ).astype(F32)

time: 71 us -> 73.5 us (1.035)
  Pallas kernels: 70.1 us -> 72.5 us
    pallas_call x1, Pallas kernels: 67.9 us -> 70.4 us  [local(): pl.pallas_call(body, out_shape=(jax.ShapeDtypeStruct(c_states.shape, F32)...]
where the time goes in v5:
time: 73.5 us; the launch traced here: 73.3 us
  Pallas kernels  72.5 us (99%)
  between operations  0.8 us (1%)
    pallas_call x1, Pallas kernels, local(): pl.pallas_call(body, out_shape=(jax.ShapeDtypeStruct(c_states.shape, F32)...  70.4 us
    pallas_call x1, Pallas kernels, local(): pl.pallas_call(place_results, out_shape=tuple((jax.ShapeDtypeStruct(value...  2.14 us

profile of v5, /device:TPU:1, one launch (start us, length us, event | category | flops | bytes accessed | tf_op | source)
XLA Modules:
  0.0 73.3 jit_solution(12537020315150547453)
XLA Ops:
  0.6 70.4 %shard_map.58 = (f32[1,64,8,128]{3,2,1,0:T(8,128)}, f32[1,64,8,128]{3,2,1,0:T(8,128)}, f32[4,64,576]{2,1,0:T(8,128)}) custom-call(f32[1,64,8,128]{3,2,1,0:T(8,128)} %x_hbm.1, f32[1,64,8,128]{3,2,1,0:T(8,128)} %q_hbm.1, bf16[4,64,576]{2,1,0:T(8,128)(2,1)} %w_hbm.1), custom_call_target="tpu_custom_call" | custom-call | tf_op jit(solution)/shard_map/pallas_call | solution.py:543
  71.0 2.1 %shard_map.59 = (f32[1,64,8,128]{3,2,1,0:T(8,128)}, f32[1,64,8,128]{3,2,1,0:T(8,128)}, f32[4,64,576]{2,1,0:T(8,128)}) custom-call(f32[1,64,8,128]{3,2,1,0:T(8,128)} %get-tuple-element.6.refs_0_, f32[1,64,8,128]{3,2,1,0:T(8,128)} %get-tuple-element.7.refs_1_, f32[4,64,576]{2,1,0:T(8,128)} %get-tuple-element.8.refs_2_), custom_call_target="tpu_custom_call" | custom-call | tf_op jit(solution)/shard_map/pallas_call | solution.py:557
